TPU v7x, 256 devices: a whole 4x4x8 slice. The times are simulated.
256 devices in a mesh: row: 8 (over x, core), col: 32 (over z, y).
Axes of the slice: x: 4, y: 4, z: 8, core: 2. Of those that a mesh axis runs over, the one named last changes fastest.
Arguments:
- pixels: float32 [224, 128, 4096], P(None, 'row', 'col'), may hold values from -6 to 6
- library: float32 [224, 4096], P(None, 'col'), may hold values from -0.375 to 0.375
- block_ids: int32 [8, 32, 2], replicated, may hold values from 0 to 31, as said below
- counts: int32 [8, 32], replicated, may hold values from 1 to 2
Outputs:
- abundance: float32 [2, 128, 128, 4096], P(None, None, 'row', 'col')
- library_grad: float32 [4096, 224], P('col')
Inputs may be any that keep to these rules, and one draw needn't show every extreme that they name: `block_ids`: the two slots of a tile name different blocks; every block is named by some tile.
All inputs are finite; a program needn't handle non-finite values.
Results may differ from a plain program's by a relative error of at most 0.00018.
Values sent between devices are 32-bit elements; how exact they have to be, the bound alone decides.
A program may use at most 64 MiB of HBM per device.

v0:
```python
import jax
import jax.numpy as jnp
from jax import lax
from jax.sharding import PartitionSpec as P

BLOCK = 128
BLOCKS = 32
ITERS = 3


step_size = 0.2
penalty = 1.0
smoothing = 0.5
threshold = 0.05


def with_halo(block, sides, width):
    for axis, dim in sides:
        count = lax.axis_size(axis)
        forward = [(i, i + 1) for i in range(count - 1)]
        backward = [(target, source) for source, target in forward]
        low = lax.ppermute(
            lax.slice_in_dim(block, block.shape[dim] - width, None, axis=dim), axis, forward
        )
        high = lax.ppermute(lax.slice_in_dim(block, 0, width, axis=dim), axis, backward)
        block = jnp.concatenate([low, block, high], axis=dim)
    return block


def local(pixels, library, block_ids, counts):
    highest_precision = lax.Precision.HIGHEST
    active = block_ids.shape[2]
    band_count = library.shape[0]
    tile_rows = pixels.shape[1]
    tile_cols = pixels.shape[2]
    pix_count = tile_rows * tile_cols
    width_total = active * BLOCK
    row_pos = lax.axis_index("row")
    col_pos = lax.axis_index("col")
    row_table = lax.dynamic_index_in_dim(block_ids, row_pos, 0, False)
    my_ids = lax.dynamic_index_in_dim(row_table, col_pos, 0, False)
    my_count = lax.dynamic_index_in_dim(
        lax.dynamic_index_in_dim(counts, row_pos, 0, False), col_pos, 0, False
    )
    in_use = (jnp.arange(active) < my_count).astype(jnp.float32)
    block_range = jnp.arange(BLOCK)
    portion = lax.all_gather(library, "col", axis=1, tiled=True)
    columns = jnp.arange(portion.shape[1])
    owners = columns // BLOCK
    within = columns % BLOCK
    selected = []
    for slot in range(active):
        onehot = (
            (owners == my_ids[slot])[:, None] & (within[:, None] == block_range[None, :])
        ).astype(jnp.float32)
        selected.append(jnp.dot(portion, onehot, precision=highest_precision))
    blocks = jnp.stack(selected)
    blocks = blocks * in_use[:, None, None]
    spectra_library = blocks.transpose(1, 0, 2).reshape(band_count, width_total)
    observed_pixels = pixels.reshape(band_count, pix_count)
    abundance = jnp.zeros((width_total, tile_rows, tile_cols), jnp.float32)
    sparse_copy = jnp.zeros_like(abundance)
    scaled_dual = jnp.zeros_like(abundance)
    for iterate in range(ITERS):
        residual_error = (
            jnp.dot(
                spectra_library,
                abundance.reshape(width_total, pix_count),
                precision=highest_precision,
            )
            - observed_pixels
        )
        gradient_field = lax.dot_general(
            spectra_library, residual_error, (((0,), (0,)), ((), ())), precision=highest_precision
        )
        padded = with_halo(abundance, (("row", 1), ("col", 2)), 1)
        beside = (
            padded[:, 2:, 1:-1] + padded[:, :-2, 1:-1] + padded[:, 1:-1, 2:] + padded[:, 1:-1, :-2]
        )
        laplace = 4.0 * abundance - beside
        abundance = abundance - step_size * (
            gradient_field.reshape(width_total, tile_rows, tile_cols)
            + penalty * (abundance - sparse_copy + scaled_dual)
            + smoothing * laplace
        )
        sparse_copy = jnp.maximum(abundance + scaled_dual - threshold, 0.0)
        scaled_dual = scaled_dual + abundance - sparse_copy
    flat_abund = abundance.reshape(width_total, pix_count)
    residual_error = (
        jnp.dot(spectra_library, flat_abund, precision=highest_precision) - observed_pixels
    )
    slot_abund = flat_abund.reshape(active, BLOCK, pix_count)
    slot_grads = jnp.einsum("abp,lp->abl", slot_abund, residual_error, precision=highest_precision)
    slot_grads = slot_grads * in_use[:, None, None] / pix_count
    per_column = BLOCKS * BLOCK // lax.axis_size("col")
    row_total = per_column * lax.axis_size("col")
    row_ids = jnp.arange(row_total)
    owners = row_ids // BLOCK
    within = row_ids % BLOCK
    summed = jnp.zeros((row_total, band_count), jnp.float32)
    for slot in range(active):
        onehot = (
            (owners == my_ids[slot])[:, None] & (within[:, None] == block_range[None, :])
        ).astype(jnp.float32)
        summed = summed + jnp.dot(onehot, slot_grads[slot], precision=highest_precision)
    partial_sum = lax.psum_scatter(summed, "col", scatter_dimension=0, tiled=True)
    library_grad = lax.psum(partial_sum, "row")
    return (abundance.reshape(active, BLOCK, tile_rows, tile_cols), library_grad)


def solution(mesh):
    placed = (P(None, "row", "col"), P(None, "col"), P(), P())
    return jax.shard_map(
        local,
        mesh=mesh,
        in_specs=placed,
        out_specs=(P(None, None, "row", "col"), P("col", None)),
        check_vma=False,
    )
```

profile of v0, /device:TPU:1, one launch (start us, length us, event | category | flops | bytes accessed | tf_op | source)
XLA Modules:
  0.0 473.1 jit_solution(18149641577648164078)
XLA Ops:
  7.2 0.0 copy-start
  7.2 0.0 all-gather.2.cloned.1.call-start
  7.2 0.7 all-gather.2.cloned.1.call-update
  7.9 0.0 reduce-scatter.2.cloned.1.call-start
  8.0 4.5 collective-permute-start.1
  12.5 1.9 collective-permute-start
  14.4 1.3 dynamic_slice.13
  15.8 0.0 copy-done
  15.8 0.1 constant_dynamic-slice_fusion
  15.8 0.5 fusion.96
  16.3 0.7 fusion.92
  17.0 0.7 fusion.91
  17.7 0.6 compare_convert_fusion
  18.3 0.0 collective-permute-done.1
  18.3 0.4 collective-permute-done
  18.8 0.2 broadcast.106
  19.0 0.0 copy-start.4
  19.0 1.3 copy-done.4
  20.3 1.3 collective-permute-start.2
  21.6 4.0 collective-permute-start.3
  25.6 66.9 %all-gather.2.cloned.1.call-done = f32[224,4096]{1,0:T(8,128)} async-done(((f32[224,128]{1,0:T(8,128)}), f32[224,4096]{1,0:T(8,128)}) %all-gather.2.cloned.1.call-update) | async-done | bytes 3670032 | tf_op jit(solution)/shard_map/all_gather | solution.py:47
  92.6 4.5 fusion.59
  97.1 0.0 copy-done.3
  97.1 0.0 copy-start.1
  97.1 2.3 fusion.62
  99.4 0.1 fusion.82
  99.5 3.3 fusion.44
  102.8 0.2 copy.12
  103.0 0.2 reshape.77
  103.2 0.0 collective-permute-done.2
  103.2 0.0 collective-permute-done.3
  103.2 7.7 %broadcast_subtract_fusion = (f32[256,16,128]{0,2,1:T(8,128)S(1)}, f32[256,16,128]{0,2,1:T(8,128)S(1)}) fusion(f32[256,16,128]{0,2,1:T(8,128)} %copy-done.4, f32[256,1,128]{0,2,1:T(8,128)S(1)} %collective-permute-done, f32[256,1,128]{0,2,1:T(8,128)S(1)} %collective-permute-done.1, f32[256,18,1]{0,2,1:T(1,128)S(1)} %collective-permute-done.3, ...), kind=kOutput, calls=%fused_computation.83 | convolution fusion | flops 1416626176 | bytes 8654848 | tf_op jit(solution)/shard_map/dot_general | solution.py:73
  110.9 6.0 %collective-permute-start.5 = (f32[256,1,128]{0,2,1:T(8,128)S(1)}, f32[256,1,128]{0,2,1:T(8,128)S(1)}, u32[]{:S(2)}, u32[]{:S(2)}) collective-permute-start(f32[256,1,128]{0,2,1:T(8,128)S(1)} %get-tuple-element.14), channel_id=1, source_target_pairs={{0,32},{32,64},{64,96},{96,128},{128,160},{160,192},{192,224},{1,3... | collective-permute-start | bytes 393224 | tf_op jit(solution)/shard_map/ppermute | solution.py:22
  117.0 1.9 collective-permute-start.4
  118.9 0.0 collective-permute-done.5
  118.9 4.3 collective-permute-done.4
  123.3 1.3 collective-permute-start.6
  124.6 4.8 %collective-permute-start.7 = (f32[256,18,1]{0,2,1:T(1,128)S(1)}, f32[256,18,1]{0,2,1:T(1,128)S(1)}, u32[]{:S(2)}, u32[]{:S(2)}) collective-permute-start(f32[256,18,1]{0,2,1:T(1,128)S(1)} %get-tuple-element.9), channel_id=1, source_target_pairs={{0,1},{1,2},{2,3},{3,4},{4,5},{5,6},{6,7},{7,8},{8,9},{9,10},{10,1... | collective-permute-start | bytes 55304 | tf_op jit(solution)/shard_map/ppermute | solution.py:22
  129.4 2.6 fusion.45
  132.0 0.0 collective-permute-done.6
  132.0 0.0 collective-permute-done.7
  132.0 4.6 fusion.21
  136.6 2.1 collective-permute-start.9
  138.7 2.3 collective-permute-start.8
  141.0 0.0 collective-permute-done.9
  141.0 4.0 collective-permute-done.8
  145.0 1.3 collective-permute-start.10
  146.3 4.3 collective-permute-start.11
  150.6 2.6 fusion.46
  153.2 0.0 collective-permute-done.10
  153.2 0.0 collective-permute-done.11
  153.3 7.5 %fusion.13 = f32[256,16,128]{0,2,1:T(8,128)} fusion(f32[256,16,128]{0,2,1:T(8,128)S(1)} %fusion.21, f32[256,18,1]{0,2,1:T(1,128)S(1)} %collective-permute-done.11, f32[256,1,128]{0,2,1:T(8,128)S(1)} %collective-permute-done.8, f32[256,1,128]{0,2,1:T(8,128)S(1)} %collective-permute-done.9, f32[256,18,1]{0,2,1:T(1,128)S(1)} %collective-permute-done.10, ...), kind=kOutput, calls=%fused_computation.21 | convolution fusion | flops 1423966208 | bytes 8654848 | tf_op jit(solution)/shard_map/dot_general | solution.py:73
  160.8 3.2 reshape_reshape.3
  164.0 4.4 fusion
  168.4 1.8 fusion.56
  170.2 2.5 fusion.28
  172.7 4.4 convolution_add_fusion
  177.1 0.0 reduce-scatter.2.cloned.1.call-update
  177.1 0.0 all-reduce.4.cloned.1.call-start
  177.1 219.9 %reduce-scatter.2.cloned.1.call-done = f32[128,224]{0,1:T(8,128)} async-done(((f32[4096,224]{0,1:T(8,128)}), f32[128,224]{0,1:T(8,128)}) %reduce-scatter.2.cloned.1.call-update) | async-done | bytes 114704 | tf_op jit(solution)/shard_map/reduce_scatter | solution.py:106
  397.0 0.0 all-reduce.4.cloned.1.call-update
  397.1 2.0 copy.20
  399.0 66.0 %all-reduce.4.cloned.1.call-done = f32[128,224]{0,1:T(8,128)} async-done(((f32[128,224]{0,1:T(8,128)}), f32[128,224]{0,1:T(8,128)}) %all-reduce.4.cloned.1.call-update) | async-done | bytes 114704 | tf_op jit(solution)/shard_map/psum | solution.py:107
  465.0 1.6 copy.73
  (13 shorter events, 0.1 us)
Async XLA Ops:
  7.2 8.6 %copy-start = (s32[8,32,2]{1,2,0:T(2,128)S(1)}, s32[8,32,2]{1,2,0:T(2,128)}, u32[]{:S(2)}) copy-start(s32[8,32,2]{1,2,0:T(2,128)} %param.6) | copy-start | bytes 6148
  7.2 85.4 %all-gather.2.cloned.1.call-start = ((), (), s32[]{:S(2)}) async-start(), calls=%async_computation.1 | async-start | bytes 3784704 | tf_op jit(solution)/shard_map/all_gather | solution.py:47
  7.9 389.1 %reduce-scatter.2.cloned.1.call-start = ((), (), s32[]{:S(2)}) async-start(), calls=%async_computation.2 | async-start | bytes 3784704 | tf_op jit(solution)/shard_map/reduce_scatter | solution.py:106
  8.0 10.3 %collective-permute-start.1 = (f32[256,1,128]{0,2,1:T(8,128)S(1)}, f32[256,1,128]{0,2,1:T(8,128)S(1)}, u32[]{:S(2)}, u32[]{:S(2)}) collective-permute-start(f32[256,1,128]{0,2,1:T(8,128)S(1)} %broadcast.107), channel_id=1, source_target_pairs={{0,32},{32,64},{64,96},{96,128},{128,160},{160,192},{192,224},{1,3... | collective-permute-start | bytes 393224 | tf_op jit(solution)/shard_map/ppermute | solution.py:22
  12.5 6.3 %collective-permute-start = (f32[256,1,128]{0,2,1:T(8,128)S(1)}, f32[256,1,128]{0,2,1:T(8,128)S(1)}, u32[]{:S(2)}, u32[]{:S(2)}) collective-permute-start(f32[256,1,128]{0,2,1:T(8,128)S(1)} %broadcast.107), channel_id=1, source_target_pairs={{32,0},{64,32},{96,64},{128,96},{160,128},{192,160},{224,192},{33,... | collective-permute-start | bytes 393224 | tf_op jit(solution)/shard_map/ppermute | solution.py:25
  19.0 1.3 copy-start.4
  20.3 82.8 %collective-permute-start.2 = (f32[256,18,1]{0,2,1:T(1,128)S(1)}, f32[256,18,1]{0,2,1:T(1,128)S(1)}, u32[]{:S(2)}, u32[]{:S(2)}) collective-permute-start(f32[256,18,1]{0,2,1:T(1,128)S(1)} %get-tuple-element.10), channel_id=1, source_target_pairs={{1,0},{2,1},{3,2},{4,3},{5,4},{6,5},{7,6},{8,7},{9,8},{10,9},{11,1... | collective-permute-start | bytes 55304 | tf_op jit(solution)/shard_map/ppermute | solution.py:25
  21.6 81.5 %collective-permute-start.3 = (f32[256,18,1]{0,2,1:T(1,128)S(1)}, f32[256,18,1]{0,2,1:T(1,128)S(1)}, u32[]{:S(2)}, u32[]{:S(2)}) collective-permute-start(f32[256,18,1]{0,2,1:T(1,128)S(1)} %get-tuple-element.11), channel_id=1, source_target_pairs={{0,1},{1,2},{2,3},{3,4},{4,5},{5,6},{6,7},{7,8},{8,9},{9,10},{10,1... | collective-permute-start | bytes 55304 | tf_op jit(solution)/shard_map/ppermute | solution.py:22
  92.6 4.5 copy-start.3
  97.1 2.4 copy-start.1
  110.9 8.0 %collective-permute-start.5 = (f32[256,1,128]{0,2,1:T(8,128)S(1)}, f32[256,1,128]{0,2,1:T(8,128)S(1)}, u32[]{:S(2)}, u32[]{:S(2)}) collective-permute-start(f32[256,1,128]{0,2,1:T(8,128)S(1)} %get-tuple-element.14), channel_id=1, source_target_pairs={{0,32},{32,64},{64,96},{96,128},{128,160},{160,192},{192,224},{1,3... | collective-permute-start | bytes 393224 | tf_op jit(solution)/shard_map/ppermute | solution.py:22
  117.0 6.3 %collective-permute-start.4 = (f32[256,1,128]{0,2,1:T(8,128)S(1)}, f32[256,1,128]{0,2,1:T(8,128)S(1)}, u32[]{:S(2)}, u32[]{:S(2)}) collective-permute-start(f32[256,1,128]{0,2,1:T(8,128)S(1)} %get-tuple-element.15), channel_id=1, source_target_pairs={{32,0},{64,32},{96,64},{128,96},{160,128},{192,160},{224,192},{33,... | collective-permute-start | bytes 393224 | tf_op jit(solution)/shard_map/ppermute | solution.py:25
  123.3 8.7 %collective-permute-start.6 = (f32[256,18,1]{0,2,1:T(1,128)S(1)}, f32[256,18,1]{0,2,1:T(1,128)S(1)}, u32[]{:S(2)}, u32[]{:S(2)}) collective-permute-start(f32[256,18,1]{0,2,1:T(1,128)S(1)} %get-tuple-element.8), channel_id=1, source_target_pairs={{1,0},{2,1},{3,2},{4,3},{5,4},{6,5},{7,6},{8,7},{9,8},{10,9},{11,1... | collective-permute-start | bytes 55304 | tf_op jit(solution)/shard_map/ppermute | solution.py:25
  124.6 7.4 %collective-permute-start.7 = (f32[256,18,1]{0,2,1:T(1,128)S(1)}, f32[256,18,1]{0,2,1:T(1,128)S(1)}, u32[]{:S(2)}, u32[]{:S(2)}) collective-permute-start(f32[256,18,1]{0,2,1:T(1,128)S(1)} %get-tuple-element.9), channel_id=1, source_target_pairs={{0,1},{1,2},{2,3},{3,4},{4,5},{5,6},{6,7},{7,8},{8,9},{9,10},{10,1... | collective-permute-start | bytes 55304 | tf_op jit(solution)/shard_map/ppermute | solution.py:22
  136.6 4.3 collective-permute-start.9
  138.7 6.3 %collective-permute-start.8 = (f32[256,1,128]{0,2,1:T(8,128)S(1)}, f32[256,1,128]{0,2,1:T(8,128)S(1)}, u32[]{:S(2)}, u32[]{:S(2)}) collective-permute-start(f32[256,1,128]{0,2,1:T(8,128)S(1)} %get-tuple-element.13), channel_id=1, source_target_pairs={{32,0},{64,32},{96,64},{128,96},{160,128},{192,160},{224,192},{33,... | collective-permute-start | bytes 393224 | tf_op jit(solution)/shard_map/ppermute | solution.py:25
  145.0 8.2 %collective-permute-start.10 = (f32[256,18,1]{0,2,1:T(1,128)S(1)}, f32[256,18,1]{0,2,1:T(1,128)S(1)}, u32[]{:S(2)}, u32[]{:S(2)}) collective-permute-start(f32[256,18,1]{0,2,1:T(1,128)S(1)} %get-tuple-element.6), channel_id=1, source_target_pairs={{1,0},{2,1},{3,2},{4,3},{5,4},{6,5},{7,6},{8,7},{9,8},{10,9},{11,1... | collective-permute-start | bytes 55304 | tf_op jit(solution)/shard_map/ppermute | solution.py:25
  146.3 6.9 %collective-permute-start.11 = (f32[256,18,1]{0,2,1:T(1,128)S(1)}, f32[256,18,1]{0,2,1:T(1,128)S(1)}, u32[]{:S(2)}, u32[]{:S(2)}) collective-permute-start(f32[256,18,1]{0,2,1:T(1,128)S(1)} %get-tuple-element.7), channel_id=1, source_target_pairs={{0,1},{1,2},{2,3},{3,4},{4,5},{5,6},{6,7},{7,8},{8,9},{9,10},{10,1... | collective-permute-start | bytes 55304 | tf_op jit(solution)/shard_map/ppermute | solution.py:22
  164.0 4.4 copy-start.5
  177.1 220.0 %copy-start.2 = (f32[256,16,128]{0,2,1:T(8,128)S(1)}, f32[256,16,128]{0,2,1:T(8,128)}, u32[]{:S(2)}) copy-start(f32[256,16,128]{0,2,1:T(8,128)} %fusion.13) | copy-start | bytes 6291460
  177.1 287.9 %all-reduce.4.cloned.1.call-start = ((), (), s32[]{:S(2)}) async-start(), calls=%async_computation.3 | async-start | bytes 229376 | tf_op jit(solution)/shard_map/psum | solution.py:107
Sparse Core Ops, SparseCore 0:
  10.5 82.0 all-gather.1
  177.2 219.7 reduce-scatter.1
  399.5 65.5 all-reduce.3
where the time goes:
time: 474 us; the launch traced here: 473 us
  waiting for transfers between devices  362 us (76%)
  matrix products  48.2 us (10%)
  starting transfers between devices  35.7 us (8%)
  between operations  14.1 us (3%)
  local copies, waits for them, and re-layouts  10.6 us (2%)
    reduce_scatter x1, waiting for transfers between devices, local(): lax.psum_scatter(summed, 'col', scatter_dimension=0, tiled=True)  220 us
    all_gather x1, waiting for transfers between devices, local(): portion = lax.all_gather(library, 'col', axis=1, tiled=True)  66.9 us
    psum x1, waiting for transfers between devices, local(): library_grad = lax.psum(partial_sum, 'row')  66 us
    ppermute x6, starting transfers between devices, with_halo(): lax.ppermute(lax.slice_in_dim(block, block.shape[dim] - width, None, axis...  25.6 us
    dot_general x3, matrix products, local(): lax.dot_general(spectra_library, residual_error, (((0,), (0,)), ((), ()))...  19.8 us
    ppermute x6, starting transfers between devices, with_halo(): lax.ppermute(lax.slice_in_dim(block, 0, width, axis=dim), axis, backward)  10 us
  transfers between devices with their start and end apart: 15, of which 6 were waited for; matrix products, arithmetic and copies ran while one was open for 5% of the time, Pallas kernels for 0%

commit v1 on v0

v1 whole, which is shorter than its diff:
```python
import functools

import jax
import jax.numpy as jnp
from jax import lax
from jax.experimental import pallas as pl
from jax.experimental.pallas import tpu as pltpu
from jax.sharding import PartitionSpec as P

MESH = pl.DeviceIdType.MESH
BANDS = 224
BLOCK = 128
SLOTS = 2
WIDE = SLOTS * BLOCK
TILE_H = 16
TILE_W = 128
PIX = TILE_H * TILE_W
PART = 32
PARTS = BANDS // PART
ROWS = 8
PAIR = 2 * TILE_W
PAIRS = PIX // PAIR
STEP = 0.2
THRESHOLD = 0.05
F32 = jnp.float32
BF16 = jnp.bfloat16


def nn(a, b):
    return lax.dot_general(a, b, (((1,), (0,)), ((), ())), preferred_element_type=F32)


def nt(a, b):
    return lax.dot_general(a, b, (((1,), (1,)), ((), ())), preferred_element_type=F32)


def split(x):
    hi = x.astype(BF16)
    return hi, (x - hi.astype(F32)).astype(BF16)


def kernel(
    cols, pix_hbm, lib, ids, counts, abund_hbm, lgrad,
    pix, lhi, llo, gath, bsend, spec, a1, a2, a3, obuf, ones, tri,
    hs, hr, gsend, grecv, gacc, gall, outt,
    send_a, recv_a, send_b, recv_b, send_h, recv_h, send_g, recv_g,
    send_t, recv_t, send_c, recv_c, sem_pix, sem_out,
):
    r = lax.axis_index("row")
    c = lax.axis_index("col")
    mine = pl.ds(pl.multiple_of(r * PART, PART), PART)

    def far(src, dst, ssem, rsem, dev):
        return pltpu.make_async_remote_copy(
            src_ref=src, dst_ref=dst, send_sem=ssem, recv_sem=rsem,
            device_id=dev, device_id_type=MESH,
        )

    pix_in = pltpu.make_async_copy(pix_hbm, pix, sem_pix)
    pix_in.start()

    barrier = pltpu.get_barrier_semaphore()

    def greet_col(k, _):
        pl.semaphore_signal(barrier, inc=1, device_id=(r, lax.rem(c + k, cols)), device_id_type=MESH)
        return 0

    def greet_row(k, _):
        pl.semaphore_signal(barrier, inc=1, device_id=(lax.rem(r + k, ROWS), c), device_id_type=MESH)
        return 0

    lax.fori_loop(1, cols, greet_col, 0)
    lax.fori_loop(1, ROWS, greet_row, 0)
    pl.semaphore_wait(barrier, cols - 1 + ROWS - 1)

    def lib_copy(k):
        return far(lib.at[mine], gath.at[c], send_a.at[k], recv_a.at[k], (r, lax.rem(c + k, cols)))

    @pl.when(r < PARTS)
    def _():
        def go(k, _):
            lib_copy(k).start()
            return 0

        lax.fori_loop(1, cols, go, 0)
        gath[c] = lib[mine, :]

    lane = lax.broadcasted_iota(jnp.int32, (64, PIX), 1)
    which = lax.rem(lax.broadcasted_iota(jnp.int32, (64, PIX), 0), 32)
    spot = jnp.where(which < TILE_H, which * TILE_W, (which - TILE_H) * TILE_W + TILE_W - 1)
    ones[...] = jnp.where(lane == spot, 1.0, 0.0).astype(BF16)
    ti = lax.broadcasted_iota(jnp.int32, (PAIR, PAIR), 0)
    tj = lax.broadcasted_iota(jnp.int32, (PAIR, PAIR), 1)
    near = (jnp.abs(ti - tj) == 1) & (ti // TILE_W == tj // TILE_W)
    tri[...] = jnp.where(near, 1.0, 0.0).astype(BF16)

    @pl.when(r == 0)
    def _():
        for a in (a1, a2):
            a[:, :TILE_W] = jnp.zeros((WIDE, TILE_W), F32)

    @pl.when(r == ROWS - 1)
    def _():
        for a in (a1, a2):
            a[:, TILE_W + PIX:] = jnp.zeros((WIDE, TILE_W), F32)

    @pl.when(c == 0)
    def _():
        for i in range(2):
            hr[i, :TILE_H] = jnp.zeros((TILE_H, WIDE), F32)

    @pl.when(c == cols - 1)
    def _():
        for i in range(2):
            hr[i, TILE_H:] = jnp.zeros((TILE_H, WIDE), F32)

    pix_in.wait()
    for h in range(TILE_H):
        hi, lo = split(pix[pl.ds(h, BANDS, TILE_H), :])
        lhi[WIDE:, h * TILE_W:(h + 1) * TILE_W] = hi
        llo[WIDE:, h * TILE_W:(h + 1) * TILE_W] = lo

    def choose(row, s):
        use = jnp.where(counts[row, c] > s, 1.0, 0.0)
        return gath[ids[row, c, s]] * use

    def spec_copy(k):
        return far(bsend.at[k], spec.at[:, mine, :], send_b.at[k], recv_b.at[r], (lax.rem(r + k, ROWS), c))

    @pl.when(r < PARTS)
    def _():
        def got(k, _):
            lib_copy(k).wait_recv()
            return 0

        lax.fori_loop(1, cols, got, 0)
        for k in range(1, ROWS):
            for s in range(SLOTS):
                bsend[k, s] = choose(lax.rem(r + k, ROWS), s)
            spec_copy(k).start()
        for s in range(SLOTS):
            spec[s, mine, :] = choose(r, s)

    for p in range(PARTS):
        @pl.when(r != p)
        def _():
            far(bsend.at[0], spec.at[:, p * PART:(p + 1) * PART, :], send_b.at[0], recv_b.at[p], (r, c)).wait_recv()

    spectra = jnp.concatenate([spec[0], spec[1]], axis=1)
    spectra_t = spectra.T
    s_hi, s_lo = split(spectra)
    w_hi, w_lo = split(STEP * spectra_t)

    def lanes(j, pad=0):
        return pl.ds(pl.multiple_of(j * PAIR + pad, TILE_W), PAIR)

    def keep(j, value):
        hi, lo = split(value)
        lhi[:WIDE, lanes(j)] = hi
        llo[:WIDE, lanes(j)] = lo

    def row_copies(i, a):
        up = far(a.at[:, TILE_W:2 * TILE_W], a.at[:, TILE_W + PIX:], send_h.at[i, 2], recv_h.at[i, 3], (r - 1, c))
        down = far(a.at[:, PIX:TILE_W + PIX], a.at[:, :TILE_W], send_h.at[i, 3], recv_h.at[i, 2], (r + 1, c))
        return up, down

    def col_copies(i):
        left = far(hs.at[i, :TILE_H], hr.at[i, TILE_H:], send_h.at[i, 0], recv_h.at[i, 1], (r, c - 1))
        right = far(hs.at[i, TILE_H:], hr.at[i, :TILE_H], send_h.at[i, 1], recv_h.at[i, 0], (r, c + 1))
        return left, right

    def edges(i, a, what):
        up, down = row_copies(i, a)
        left, right = col_copies(i)

        @pl.when(c > 0)
        def _():
            if what == "start":
                left.start()
            elif what == "send":
                left.wait_send()
            else:
                right.wait_recv()

        @pl.when(c < cols - 1)
        def _():
            if what == "start":
                right.start()
            elif what == "send":
                right.wait_send()
            else:
                left.wait_recv()

        @pl.when(r > 0)
        def _():
            if what == "start":
                up.start()
            elif what == "send":
                up.wait_send()
            else:
                down.wait_recv()

        @pl.when(r < ROWS - 1)
        def _():
            if what == "start":
                down.start()
            elif what == "send":
                down.wait_send()
            else:
                up.wait_recv()

    def pack(i):
        picked = ones[:32, :]
        hs[i] = nt(picked, lhi[:WIDE, :]) + nt(picked, llo[:WIDE, :])

    def first(j, _):
        p_hi = lhi[WIDE:, lanes(j)]
        p_lo = llo[WIDE:, lanes(j)]
        value = nn(w_hi, p_hi) + nn(w_hi, p_lo) + nn(w_lo, p_hi)
        a1[:, lanes(j, TILE_W)] = value
        keep(j, value)
        return 0

    lax.fori_loop(0, PAIRS, first, 0)
    pack(0)
    edges(0, a1, "start")

    t_hi, t_lo = split(spectra_t)
    gram = nn(t_hi, s_hi) + nn(t_hi, s_lo) + nn(t_lo, s_hi)
    gi = lax.broadcasted_iota(jnp.int32, (WIDE, WIDE), 0)
    gj = lax.broadcasted_iota(jnp.int32, (WIDE, WIDE), 1)
    update = jnp.where(gi == gj, 0.4, 0.0) - STEP * gram
    u_hi, u_lo = split(update)

    def inner(j, now, excess):
        a_hi = lhi[:WIDE, lanes(j)]
        a_lo = llo[:WIDE, lanes(j)]
        value = nn(u_hi, a_hi) + nn(u_hi, a_lo) + nn(u_lo, a_hi)
        beside = nn(a_hi, tri[...]) + nn(a_lo, tri[...])
        value = value + a1[:, lanes(j, TILE_W)] + STEP * (jnp.abs(excess) - THRESHOLD)
        return value, beside

    def middle(j, now):
        above = now[:, lanes(j)]
        below = now[:, lanes(j, 2 * TILE_W)]
        return above, below

    def second(j, _):
        own = a1[:, lanes(j, TILE_W)]
        value, beside = inner(j, a1, own - THRESHOLD)
        a2[:, lanes(j, TILE_W)] = value + 0.1 * beside
        return 0

    def third(j, _):
        own = a2[:, lanes(j, TILE_W)]
        excess = own + jnp.minimum(a1[:, lanes(j, TILE_W)] - THRESHOLD, 0.0)
        value, beside = inner(j, a2, excess)
        a3[:, lanes(j)] = value + 0.1 * beside
        return 0

    def columns(i):
        hi, lo = split(hr[i])
        return jnp.concatenate([hi.astype(F32), lo.astype(F32)], axis=0).T.astype(BF16)

    lax.fori_loop(0, PAIRS, second, 0)
    edges(0, a1, "recv")
    side1 = columns(0)

    def second_end(j, _):
        above, below = middle(j, a1)
        value = a2[:, lanes(j, TILE_W)] + 0.1 * (nn(side1, ones[:, lanes(j)]) + above + below)
        a2[:, lanes(j, TILE_W)] = value
        keep(j, value)
        return 0

    lax.fori_loop(0, PAIRS, second_end, 0)
    pack(1)
    edges(1, a2, "start")
    lax.fori_loop(0, PAIRS, third, 0)
    edges(1, a2, "recv")
    side2 = columns(1)

    def third_end(j, _):
        above, below = middle(j, a2)
        value = a3[:, lanes(j)] + 0.1 * (nn(side2, ones[:, lanes(j)]) + above + below)
        a3[:, lanes(j)] = value
        keep(j, value)
        return 0

    lax.fori_loop(0, PAIRS, third_end, 0)
    for h in range(TILE_H):
        obuf[pl.ds(h, WIDE, TILE_H), :] = a3[:, h * TILE_W:(h + 1) * TILE_W]
    out = pltpu.make_async_copy(obuf, abund_hbm, sem_out)
    out.start()

    both = (
        nt(lhi[...], lhi[:WIDE, :]) + nt(lhi[...], llo[:WIDE, :]) + nt(llo[...], lhi[:WIDE, :])
    )
    c_hi, c_lo = split(both[:WIDE])
    grad = nn(s_hi, c_hi) + nn(s_hi, c_lo) + nn(s_lo, c_hi) - both[WIDE:]
    for s in range(SLOTS):
        use = jnp.where(counts[r, c] > s, 1.0 / PIX, 0.0)
        gsend[s] = grad[:, s * BLOCK:(s + 1) * BLOCK] * use

    def grad_copy(p):
        return far(
            gsend.at[:, p * PART:(p + 1) * PART, :], grecv.at[r], send_g.at[p], recv_g.at[r], (p, c)
        )

    for p in range(PARTS):
        @pl.when(r != p)
        def _():
            grad_copy(p).start()

        @pl.when(r == p)
        def _():
            grecv[r] = gsend[:, p * PART:(p + 1) * PART, :]

    def owner_copy(k):
        owner = lax.rem(c + k, cols)
        return far(gacc.at[owner], gall.at[k], send_t.at[k], recv_t.at[k], (r, owner))

    def part_copy(k):
        return far(outt.at[mine], outt.at[mine], send_c.at[k], recv_c.at[r], (lax.rem(r + k, ROWS), c))

    def collect(owner):
        total = jnp.zeros((PART, BLOCK), F32)
        for q in range(ROWS):
            for s in range(SLOTS):
                total = total + jnp.where(ids[q, c, s] == owner, 1.0, 0.0) * grecv[q, s]
        gacc[owner] = total

    @pl.when(r < PARTS)
    def _():
        for q in range(ROWS):
            @pl.when(r != q)
            def _():
                far(gsend.at[:, :PART, :], grecv.at[q], send_g.at[0], recv_g.at[q], (q, c)).wait_recv()

        def go(k, _):
            collect(lax.rem(c + k, cols))
            owner_copy(k).start()
            return 0

        lax.fori_loop(1, cols, go, 0)
        collect(c)

        def take(k, total):
            owner_copy(k).wait_recv()
            return total + gall[k]

        outt[mine, :] = lax.fori_loop(1, cols, take, gacc[c])
        for k in range(1, ROWS):
            part_copy(k).start()

    for p in range(PARTS):
        @pl.when(r != p)
        def _():
            block = outt.at[p * PART:(p + 1) * PART]
            far(block, block, send_c.at[0], recv_c.at[p], (r, c)).wait_recv()

    lgrad[...] = outt[...].T

    @pl.when(r < PARTS)
    def _():
        def left(k, _):
            lib_copy(k).wait_send()
            owner_copy(k).wait_send()
            return 0

        lax.fori_loop(1, cols, left, 0)
        for k in range(1, ROWS):
            spec_copy(k).wait_send()
            part_copy(k).wait_send()

    for p in range(PARTS):
        @pl.when(r != p)
        def _():
            grad_copy(p).wait_send()

    edges(0, a1, "send")
    edges(1, a2, "send")
    out.wait()


def local(cols, pixels, library, block_ids, counts):
    dma = pltpu.SemaphoreType.DMA
    abundance, grad = pl.pallas_call(
        functools.partial(kernel, cols),
        out_shape=(
            jax.ShapeDtypeStruct((WIDE * TILE_H, TILE_W), F32),
            jax.ShapeDtypeStruct((BLOCK, BANDS), F32),
        ),
        in_specs=[
            pl.BlockSpec(memory_space=pl.ANY),
            pl.BlockSpec(memory_space=pltpu.VMEM),
            pl.BlockSpec(memory_space=pltpu.SMEM),
            pl.BlockSpec(memory_space=pltpu.SMEM),
        ],
        out_specs=(
            pl.BlockSpec(memory_space=pl.ANY),
            pl.BlockSpec(memory_space=pltpu.VMEM),
        ),
        scratch_shapes=[
            pltpu.VMEM((BANDS * TILE_H, TILE_W), F32),
            pltpu.VMEM((WIDE + BANDS, PIX), BF16),
            pltpu.VMEM((WIDE + BANDS, PIX), BF16),
            pltpu.VMEM((cols, PART, BLOCK), F32),
            pltpu.VMEM((ROWS, SLOTS, PART, BLOCK), F32),
            pltpu.VMEM((SLOTS, BANDS, BLOCK), F32),
            pltpu.VMEM((WIDE, PIX + 2 * TILE_W), F32),
            pltpu.VMEM((WIDE, PIX + 2 * TILE_W), F32),
            pltpu.VMEM((WIDE, PIX), F32),
            pltpu.VMEM((WIDE * TILE_H, TILE_W), F32),
            pltpu.VMEM((64, PIX), BF16),
            pltpu.VMEM((PAIR, PAIR), BF16),
            pltpu.VMEM((2, 32, WIDE), F32),
            pltpu.VMEM((2, 32, WIDE), F32),
            pltpu.VMEM((SLOTS, BANDS, BLOCK), F32),
            pltpu.VMEM((ROWS, SLOTS, PART, BLOCK), F32),
            pltpu.VMEM((cols, PART, BLOCK), F32),
            pltpu.VMEM((cols, PART, BLOCK), F32),
            pltpu.VMEM((BANDS, BLOCK), F32),
            dma((cols,)), dma((cols,)),
            dma((ROWS,)), dma((ROWS,)),
            dma((2, 4)), dma((2, 4)),
            dma((ROWS,)), dma((ROWS,)),
            dma((cols,)), dma((cols,)),
            dma((ROWS,)), dma((ROWS,)),
            dma, dma,
        ],
        compiler_params=pltpu.CompilerParams(
            collective_id=0, has_side_effects=True, vmem_limit_bytes=48 * 1024 * 1024
        ),
    )(pixels.reshape(BANDS * TILE_H, TILE_W), library, block_ids, counts)
    return abundance.reshape(SLOTS, BLOCK, TILE_H, TILE_W), grad


def solution(mesh):
    placed = (P(None, "row", "col"), P(None, "col"), P(), P())
    return jax.shard_map(
        functools.partial(local, mesh.shape["col"]),
        mesh=mesh,
        in_specs=placed,
        out_specs=(P(None, None, "row", "col"), P("col", None)),
        check_vma=False,
    )
```

time: 474 us -> 86.1 us (0.18)
  waiting for transfers between devices: 362 us -> 0 us
  Pallas kernels: 0 us -> 79.3 us
  matrix products: 48.2 us -> 0 us
  starting transfers between devices: 35.7 us -> 0 us
  between operations: 14.1 us -> 0.64 us
    reduce_scatter x1 -> x0, waiting for transfers between devices: 220 us -> none  [local(): lax.psum_scatter(summed, 'col', scatter_dimension=0, tiled=True)]
    pallas_call x0 -> x1, Pallas kernels: none -> 79.3 us  [local(): pl.pallas_call(functools.partial(kernel, cols), out_shape=(jax.ShapeDtype...]
    all_gather x1 -> x0, waiting for transfers between devices: 66.9 us -> none  [local(): portion = lax.all_gather(library, 'col', axis=1, tiled=True)]
    psum x1 -> x0, waiting for transfers between devices: 66 us -> none  [local(): library_grad = lax.psum(partial_sum, 'row')]
    dot_general x12 -> x0, matrix products: 48.2 us -> none  [the longest x3 19.8 us: local(): lax.dot_general(spectra_library, residual_error, (((0,), (0,)), ((), ()))...]
    ppermute x12 -> x0, starting transfers between devices: 35.6 us -> none  [the longest x6 25.6 us: with_halo(): lax.ppermute(lax.slice_in_dim(block, block.shape[dim] - width, None, axis...]
    ppermute x12 -> x0, waiting for transfers between devices: 8.82 us -> none  [the longest x6 8.81 us: with_halo(): lax.ppermute(lax.slice_in_dim(block, 0, width, axis=dim), axis, backward)]
  transfers between devices with their start and end apart: 15 -> 0, of which waited for: 6 -> 0; matrix products, arithmetic and copies ran while one was open for 5% -> 0% of each run, Pallas kernels for 0% -> 0%
where the time goes in v1:
time: 86.1 us; the launch traced here: 85.9 us
  Pallas kernels  79.3 us (92%)
  local copies, waits for them, and re-layouts  5.97 us (7%)
    pallas_call x1, Pallas kernels, local(): pl.pallas_call(functools.partial(kernel, cols), out_shape=(jax.ShapeDtype...  79.3 us
    unnamed x9, local copies, waits for them, and re-layouts  5.97 us

profile of v1, /device:TPU:1, one launch (start us, length us, event | category | flops | bytes accessed | tf_op | source)
XLA Modules:
  0.0 85.9 jit_solution(7984707617043048724)
XLA Ops:
  0.6 0.8 copy.6.ids
  1.5 0.0 copy-start
  1.5 1.5 %copy-done = f32[224,16,128]{2,1,0:T(8,128)S(1)} copy-done((f32[224,16,128]{2,1,0:T(8,128)S(1)}, f32[224,16,128]{2,1,0:T(8,128)}, u32[]{:S(2)}) %copy-start) | copy-done | bytes 1835032
  3.0 0.0 copy-start.1
  3.0 0.9 %copy-done.1 = f32[224,128]{1,0:T(8,128)S(1)} copy-done((f32[224,128]{1,0:T(8,128)S(1)}, f32[224,128]{1,0:T(8,128)}, u32[]{:S(2)}) %copy-start.1) | copy-done | bytes 114712
  3.9 0.0 copy-start.2
  3.9 0.7 copy-done.2
  4.5 79.3 %shard_map.59 = (f32[4096,128]{1,0:T(8,128)S(1)}, f32[128,224]{1,0:T(8,128)S(1)}) custom-call(f32[3584,128]{1,0:T(8,128)S(1)} %bitcast.3, f32[224,128]{1,0:T(8,128)S(1)} %copy-done.1, s32[8,32,2]{2,1,0:T(8,128)S(1)} %copy.6.ids, s32[8,32]{1,0:T(8,128)S(1)} %copy-done.2), custom_call_target="tpu_custom_call" | custom-call | tf_op jit(solution)/shard_map/pallas_call | solution.py:388
  83.8 0.7 copy.7
  84.6 1.3 %copy.9 = f32[2,128,16,128]{3,2,1,0:T(8,128)} copy(f32[2,128,16,128]{3,2,1,0:T(8,128)S(1)} %bitcast.2) | data formatting | bytes 4194304
Async XLA Ops:
  1.5 1.5 %copy-start = (f32[224,16,128]{2,1,0:T(8,128)S(1)}, f32[224,16,128]{2,1,0:T(8,128)}, u32[]{:S(2)}) copy-start(f32[224,16,128]{2,1,0:T(8,128)} %param.4) | copy-start | bytes 5505028
  3.0 0.9 %copy-start.1 = (f32[224,128]{1,0:T(8,128)S(1)}, f32[224,128]{1,0:T(8,128)}, u32[]{:S(2)}) copy-start(f32[224,128]{1,0:T(8,128)} %lib.1) | copy-start | bytes 344068
  3.9 0.7 copy-start.2

commit v2 on v1

v2 whole, which is shorter than its diff:
```python
import functools

import jax
import jax.numpy as jnp
from jax import lax
from jax.experimental import pallas as pl
from jax.experimental.pallas import tpu as pltpu
from jax.sharding import PartitionSpec as P

MESH = pl.DeviceIdType.MESH
BANDS = 224
BLOCK = 128
SLOTS = 2
WIDE = SLOTS * BLOCK
TILE_H = 16
TILE_W = 128
PIX = TILE_H * TILE_W
PART = 32
PARTS = BANDS // PART
ROWS = 8
YS = 4
PAIR = 2 * TILE_W
PAIRS = PIX // PAIR
STEP = 0.2
THRESHOLD = 0.05
F32 = jnp.float32
BF16 = jnp.bfloat16


def nn(a, b):
    return lax.dot_general(a, b, (((1,), (0,)), ((), ())), preferred_element_type=F32)


def nt(a, b):
    return lax.dot_general(a, b, (((1,), (1,)), ((), ())), preferred_element_type=F32)


def split(x):
    hi = x.astype(BF16)
    return hi, (x - hi.astype(F32)).astype(BF16)


def kernel(
    cols, pix_hbm, lib_hbm, ids_hbm, counts_hbm, abund, lgrad,
    pix, ids, counts, lhi, llo, gath, bsend, spec, a1, a2, a3, ones,
    hs, hr, gsend, grecv, gacc, gy, gzs, gz,
    send_z, recv_z, send_y, recv_y, send_b, recv_b, send_h, recv_h, send_g, recv_g,
    send_ty, recv_ty, send_tz, recv_tz, send_c, recv_c, sem_in,
):
    ny = YS
    nz = cols // ny
    r = lax.axis_index("row")
    c = lax.axis_index("col")
    z = c // ny
    y = lax.rem(c, ny)
    mine = pl.ds(pl.multiple_of(r * PART, PART), PART)
    near_first = sorted(range(1, nz), key=lambda d: (min(d, nz - d), d))

    def far(src, dst, ssem, rsem, dev):
        return pltpu.make_async_remote_copy(
            src_ref=src, dst_ref=dst, send_sem=ssem, recv_sem=rsem,
            device_id=dev, device_id_type=MESH,
        )

    def on_z(d):
        return (r, lax.rem(z + d, nz) * ny + y)

    def on_y(e):
        return (r, z * ny + lax.rem(y + e, ny))

    def on_row(k):
        return (lax.rem(r + k, ROWS), c)

    pix_in = pltpu.make_async_copy(pix_hbm, pix, sem_in.at[0])
    ids_in = pltpu.make_async_copy(ids_hbm, ids, sem_in.at[1])
    counts_in = pltpu.make_async_copy(counts_hbm, counts, sem_in.at[2])

    @pl.when(r < PARTS)
    def _():
        pltpu.make_async_copy(lib_hbm.at[mine], gath.at[y, 0], sem_in.at[3]).start()

    ids_in.start()
    counts_in.start()
    pix_in.start()

    barrier = pltpu.get_barrier_semaphore()

    def greet(dev):
        pl.semaphore_signal(barrier, inc=1, device_id=dev, device_id_type=MESH)

    for d in range(1, nz):
        greet(on_z(d))
    for e in range(1, ny):
        greet(on_y(e))
    for k in range(1, ROWS):
        greet(on_row(k))

    @pl.when(c > 0)
    def _():
        greet((r, c - 1))

    @pl.when(c < cols - 1)
    def _():
        greet((r, c + 1))

    beside_cols = (c > 0).astype(jnp.int32) + (c < cols - 1).astype(jnp.int32)
    pl.semaphore_wait(barrier, nz - 1 + ny - 1 + ROWS - 1 + beside_cols)

    def lib_z(d):
        return far(gath.at[y, 0], gath.at[y, d], send_z.at[d], recv_z.at[d], on_z(d))

    def lib_y(d, e):
        block = gath.at[y, d]
        return far(block, block, send_y.at[d, e], recv_y.at[d, e], on_y(e))

    @pl.when(r < PARTS)
    def _():
        pltpu.make_async_copy(lib_hbm.at[mine], gath.at[y, 0], sem_in.at[3]).wait()
        for d in near_first:
            lib_z(d).start()
        for e in range(1, ny):
            lib_y(0, e).start()

    lane = lax.broadcasted_iota(jnp.int32, (64, PIX), 1)
    which = lax.rem(lax.broadcasted_iota(jnp.int32, (64, PIX), 0), 32)
    spot = jnp.where(which < TILE_H, which * TILE_W, (which - TILE_H) * TILE_W + TILE_W - 1)
    ones[...] = jnp.where(lane == spot, 1.0, 0.0).astype(BF16)

    @pl.when(r == 0)
    def _():
        for a in (a1, a2):
            a[:, :TILE_W] = jnp.zeros((WIDE, TILE_W), F32)

    @pl.when(r == ROWS - 1)
    def _():
        for a in (a1, a2):
            a[:, TILE_W + PIX:] = jnp.zeros((WIDE, TILE_W), F32)

    @pl.when(c == 0)
    def _():
        for i in range(2):
            hr[i, :TILE_H] = jnp.zeros((TILE_H, WIDE), F32)

    @pl.when(c == cols - 1)
    def _():
        for i in range(2):
            hr[i, TILE_H:] = jnp.zeros((TILE_H, WIDE), F32)

    pix_in.wait()
    for h in range(TILE_H):
        hi, lo = split(pix[pl.ds(h, BANDS, TILE_H), :])
        lhi[WIDE:, h * TILE_W:(h + 1) * TILE_W] = hi
        llo[WIDE:, h * TILE_W:(h + 1) * TILE_W] = lo
    ids_in.wait()
    counts_in.wait()

    def choose(row, s):
        block = ids[row, s, c]
        use = jnp.where(counts[row, c] > s, 1.0, 0.0)
        return gath[lax.rem(block, ny), lax.rem(z - block // ny + nz, nz)] * use

    def spec_copy(k):
        return far(bsend.at[k], spec.at[:, mine, :], send_b.at[k], recv_b.at[r], on_row(k))

    @pl.when(r < PARTS)
    def _():
        for d in near_first:
            lib_z(d).wait_recv()
            for e in range(1, ny):
                lib_y(d, e).start()
        for d in [0] + near_first:
            for e in range(1, ny):
                lib_y(d, e).wait_recv()
        for k in range(1, ROWS):
            for s in range(SLOTS):
                bsend[k, s] = choose(lax.rem(r + k, ROWS), s)
            spec_copy(k).start()
        for s in range(SLOTS):
            spec[s, mine, :] = choose(r, s)

    for p in range(PARTS):
        @pl.when(r != p)
        def _():
            far(bsend.at[0], spec.at[:, p * PART:(p + 1) * PART, :], send_b.at[0], recv_b.at[p], (r, c)).wait_recv()

    spectra = jnp.concatenate([spec[0], spec[1]], axis=1)
    s_hi, s_lo = split(spectra)
    t_hi, t_lo = split(spectra.T)

    def lanes(j, pad=0):
        return slice(j * PAIR + pad, (j + 1) * PAIR + pad)

    def keep(j, value):
        hi, lo = split(value)
        lhi[:WIDE, lanes(j)] = hi
        llo[:WIDE, lanes(j)] = lo

    def row_copies(i, a):
        up = far(a.at[:, TILE_W:2 * TILE_W], a.at[:, TILE_W + PIX:], send_h.at[i, 2], recv_h.at[i, 3], (r - 1, c))
        down = far(a.at[:, PIX:TILE_W + PIX], a.at[:, :TILE_W], send_h.at[i, 3], recv_h.at[i, 2], (r + 1, c))
        return up, down

    def col_copies(i):
        left = far(hs.at[i, :TILE_H], hr.at[i, TILE_H:], send_h.at[i, 0], recv_h.at[i, 1], (r, c - 1))
        right = far(hs.at[i, TILE_H:], hr.at[i, :TILE_H], send_h.at[i, 1], recv_h.at[i, 0], (r, c + 1))
        return left, right

    def act(low, high, pos, count, what):
        @pl.when(pos > 0)
        def _():
            if what == "start":
                low.start()
            elif what == "send":
                low.wait_send()
            else:
                high.wait_recv()

        @pl.when(pos < count - 1)
        def _():
            if what == "start":
                high.start()
            elif what == "send":
                high.wait_send()
            else:
                low.wait_recv()

    def edge_rows(i, a, what):
        act(*row_copies(i, a), r, ROWS, what)

    def edge_cols(i, what):
        act(*col_copies(i), c, cols, what)

    def pack(i):
        picked = ones[:32, :]
        hs[i] = nt(picked, lhi[:WIDE, :]) + nt(picked, llo[:WIDE, :])

    ends_first = [0, PAIRS - 1] + list(range(1, PAIRS - 1))

    for j in ends_first:
        p_hi = lhi[WIDE:, lanes(j)]
        p_lo = llo[WIDE:, lanes(j)]
        value = STEP * (nn(t_hi, p_hi) + nn(t_hi, p_lo) + nn(t_lo, p_hi))
        a1[:, lanes(j, TILE_W)] = value
        keep(j, value)
        if j == PAIRS - 1:
            edge_rows(0, a1, "start")
    pack(0)
    edge_cols(0, "start")

    gram = nn(t_hi, s_hi) + nn(t_hi, s_lo) + nn(t_lo, s_hi)
    gi = lax.broadcasted_iota(jnp.int32, (WIDE, WIDE), 0)
    gj = lax.broadcasted_iota(jnp.int32, (WIDE, WIDE), 1)
    u_hi, u_lo = split(jnp.where(gi == gj, 0.4, 0.0) - STEP * gram)
    column = lax.broadcasted_iota(jnp.int32, (WIDE, TILE_W), 1)

    def beside(own):
        halves = []
        for q in range(2):
            x = own[:, q * TILE_W:(q + 1) * TILE_W]
            from_left = jnp.where(column == 0, 0.0, pltpu.roll(x, 1, 1))
            from_right = jnp.where(column == TILE_W - 1, 0.0, pltpu.roll(x, TILE_W - 1, 1))
            halves.append(from_left + from_right)
        return jnp.concatenate(halves, axis=1)

    def inner(j, own, excess):
        a_hi = lhi[:WIDE, lanes(j)]
        a_lo = llo[:WIDE, lanes(j)]
        value = nn(u_hi, a_hi) + nn(u_hi, a_lo) + nn(u_lo, a_hi)
        value = value + a1[:, lanes(j, TILE_W)] + STEP * (jnp.abs(excess) - THRESHOLD)
        return value + 0.1 * beside(own)

    def columns(i):
        hi, lo = split(hr[i])
        return jnp.concatenate([hi.astype(F32), lo.astype(F32)], axis=0).T.astype(BF16)

    def outer(j, side, a):
        return 0.1 * (nn(side, ones[:, lanes(j)]) + a[:, lanes(j)] + a[:, lanes(j, 2 * TILE_W)])

    for j in range(PAIRS):
        own = a1[:, lanes(j, TILE_W)]
        a2[:, lanes(j, TILE_W)] = inner(j, own, own - THRESHOLD)
    edge_rows(0, a1, "recv")
    edge_cols(0, "recv")
    side1 = columns(0)
    for j in ends_first:
        value = a2[:, lanes(j, TILE_W)] + outer(j, side1, a1)
        a2[:, lanes(j, TILE_W)] = value
        keep(j, value)
        if j == PAIRS - 1:
            edge_rows(1, a2, "start")
    pack(1)
    edge_cols(1, "start")
    for j in range(PAIRS):
        own = a2[:, lanes(j, TILE_W)]
        excess = own + jnp.minimum(a1[:, lanes(j, TILE_W)] - THRESHOLD, 0.0)
        a3[:, lanes(j)] = inner(j, own, excess)
    edge_rows(1, a2, "recv")
    edge_cols(1, "recv")
    side2 = columns(1)
    for j in range(PAIRS):
        value = a3[:, lanes(j)] + outer(j, side2, a2)
        a3[:, lanes(j)] = value
        keep(j, value)

    both = (
        nt(lhi[...], lhi[:WIDE, :]) + nt(lhi[...], llo[:WIDE, :]) + nt(llo[...], lhi[:WIDE, :])
    )
    c_hi, c_lo = split(both[:WIDE])
    grad = nn(s_hi, c_hi) + nn(s_hi, c_lo) + nn(s_lo, c_hi) - both[WIDE:]
    for s in range(SLOTS):
        use = jnp.where(counts[r, c] > s, 1.0 / PIX, 0.0)
        gsend[s] = grad[:, s * BLOCK:(s + 1) * BLOCK] * use

    def grad_copy(p):
        return far(
            gsend.at[:, p * PART:(p + 1) * PART, :], grecv.at[r], send_g.at[p], recv_g.at[r], (p, c)
        )

    for p in range(PARTS):
        @pl.when(r != p)
        def _():
            grad_copy(p).start()

        @pl.when(r == p)
        def _():
            grecv[r] = gsend[:, p * PART:(p + 1) * PART, :]

    for h in range(TILE_H):
        abund[pl.ds(h, WIDE, TILE_H), :] = a3[:, h * TILE_W:(h + 1) * TILE_W]

    def sum_y(d, e):
        return far(gacc.at[e, d], gy.at[e, d], send_ty.at[d, e], recv_ty.at[d, e], on_y(e))

    def sum_z(d):
        return far(gzs.at[d], gz.at[d], send_tz.at[d], recv_tz.at[d], on_z(d))

    def part_copy(k):
        return far(lgrad.at[mine], lgrad.at[mine], send_c.at[k], recv_c.at[r], on_row(k))

    far_first = near_first[::-1] + [0]

    @pl.when(r < PARTS)
    def _():
        for q in range(ROWS):
            @pl.when(r != q)
            def _():
                far(gsend.at[:, :PART, :], grecv.at[q], send_g.at[0], recv_g.at[q], (q, c)).wait_recv()

        named = [[ids[q, s, c] for s in range(SLOTS)] for q in range(ROWS)]
        for d in far_first:
            for e in list(range(1, ny)) + [0]:
                owner = lax.rem(z + d, nz) * ny + lax.rem(y + e, ny)
                total = jnp.zeros((PART, BLOCK), F32)
                for q in range(ROWS):
                    for s in range(SLOTS):
                        total = total + jnp.where(named[q][s] == owner, 1.0, 0.0) * grecv[q, s]
                gacc[e, d] = total
                if e:
                    sum_y(d, e).start()
        for d in far_first:
            total = gacc[0, d]
            for e in range(1, ny):
                sum_y(d, e).wait_recv()
                total = total + gy[e, d]
            if d:
                gzs[d] = total
                sum_z(d).start()
        for d in near_first[::-1]:
            sum_z(d).wait_recv()
            total = total + gz[d]
        lgrad[mine, :] = total
        for k in range(1, ROWS):
            part_copy(k).start()

    for p in range(PARTS):
        @pl.when(r != p)
        def _():
            block = lgrad.at[p * PART:(p + 1) * PART]
            far(block, block, send_c.at[0], recv_c.at[p], (r, c)).wait_recv()

    @pl.when(r < PARTS)
    def _():
        for d in range(nz):
            if d:
                lib_z(d).wait_send()
                sum_z(d).wait_send()
            for e in range(1, ny):
                lib_y(d, e).wait_send()
                sum_y(d, e).wait_send()
        for k in range(1, ROWS):
            spec_copy(k).wait_send()
            part_copy(k).wait_send()

    for p in range(PARTS):
        @pl.when(r != p)
        def _():
            grad_copy(p).wait_send()

    for i, a in enumerate((a1, a2)):
        edge_rows(i, a, "send")
        edge_cols(i, "send")


def local(cols, pixels, library, block_ids, counts):
    dma = pltpu.SemaphoreType.DMA
    ny = YS
    nz = cols // ny
    hbm = pl.BlockSpec(memory_space=pltpu.HBM)
    vmem = pl.BlockSpec(memory_space=pltpu.VMEM)
    abundance, grad = pl.pallas_call(
        functools.partial(kernel, cols),
        out_shape=(
            jax.ShapeDtypeStruct((WIDE * TILE_H, TILE_W), F32),
            jax.ShapeDtypeStruct((BANDS, BLOCK), F32),
        ),
        in_specs=[hbm] * 4,
        out_specs=(vmem, vmem),
        scratch_shapes=[
            pltpu.VMEM((BANDS * TILE_H, TILE_W), F32),
            pltpu.SMEM((ROWS, SLOTS, cols), jnp.int32),
            pltpu.SMEM((ROWS, cols), jnp.int32),
            pltpu.VMEM((WIDE + BANDS, PIX), BF16),
            pltpu.VMEM((WIDE + BANDS, PIX), BF16),
            pltpu.VMEM((ny, nz, PART, BLOCK), F32),
            pltpu.VMEM((ROWS, SLOTS, PART, BLOCK), F32),
            pltpu.VMEM((SLOTS, BANDS, BLOCK), F32),
            pltpu.VMEM((WIDE, PIX + 2 * TILE_W), F32),
            pltpu.VMEM((WIDE, PIX + 2 * TILE_W), F32),
            pltpu.VMEM((WIDE, PIX), F32),
            pltpu.VMEM((64, PIX), BF16),
            pltpu.VMEM((2, 32, WIDE), F32),
            pltpu.VMEM((2, 32, WIDE), F32),
            pltpu.VMEM((SLOTS, BANDS, BLOCK), F32),
            pltpu.VMEM((ROWS, SLOTS, PART, BLOCK), F32),
            pltpu.VMEM((ny, nz, PART, BLOCK), F32),
            pltpu.VMEM((ny, nz, PART, BLOCK), F32),
            pltpu.VMEM((nz, PART, BLOCK), F32),
            pltpu.VMEM((nz, PART, BLOCK), F32),
            dma((nz,)), dma((nz,)),
            dma((nz, ny)), dma((nz, ny)),
            dma((ROWS,)), dma((ROWS,)),
            dma((2, 4)), dma((2, 4)),
            dma((ROWS,)), dma((ROWS,)),
            dma((nz, ny)), dma((nz, ny)),
            dma((nz,)), dma((nz,)),
            dma((ROWS,)), dma((ROWS,)),
            dma((4,)),
        ],
        compiler_params=pltpu.CompilerParams(
            collective_id=0, has_side_effects=True, vmem_limit_bytes=48 * 1024 * 1024
        ),
    )(
        pixels.reshape(BANDS * TILE_H, TILE_W), library,
        block_ids.transpose(0, 2, 1), counts,
    )
    return abundance.reshape(SLOTS, BLOCK, TILE_H, TILE_W), grad.T


def solution(mesh):
    placed = (P(None, "row", "col"), P(None, "col"), P(), P())
    return jax.shard_map(
        functools.partial(local, mesh.shape["col"]),
        mesh=mesh,
        in_specs=placed,
        out_specs=(P(None, None, "row", "col"), P("col", None)),
        check_vma=False,
    )
```

time: 86.1 us -> 66.3 us (0.77)
  Pallas kernels: 79.3 us -> 59.7 us
    pallas_call x1, Pallas kernels: 79.3 us -> 59.7 us  [local(): pl.pallas_call(functools.partial(kernel, cols), out_shape=(jax.ShapeDtype...]
    unnamed x9 -> x10, local copies, waits for them, and re-layouts: 5.97 us -> 5.74 us
where the time goes in v2:
time: 66.3 us; the launch traced here: 66.1 us
  Pallas kernels  59.7 us (90%)
  local copies, waits for them, and re-layouts  5.74 us (9%)
    pallas_call x1, Pallas kernels, local(): pl.pallas_call(functools.partial(kernel, cols), out_shape=(jax.ShapeDtype...  59.7 us
    unnamed x10, local copies, waits for them, and re-layouts  5.74 us

profile of v2, /device:TPU:1, one launch (start us, length us, event | category | flops | bytes accessed | tf_op | source)
XLA Modules:
  0.0 66.1 jit_solution(5514483350937568995)
XLA Ops:
  0.6 0.0 copy-start
  0.6 1.5 %copy-done = f32[224,16,128]{2,1,0:T(8,128)S(1)} copy-done((f32[224,16,128]{2,1,0:T(8,128)S(1)}, f32[224,16,128]{2,1,0:T(8,128)}, u32[]{:S(2)}) %copy-start) | copy-done | bytes 1835032
  2.1 0.0 copy-start.1
  2.1 0.9 %copy-done.1 = f32[224,128]{1,0:T(8,128)S(1)} copy-done((f32[224,128]{1,0:T(8,128)S(1)}, f32[224,128]{1,0:T(8,128)}, u32[]{:S(2)}) %copy-start.1) | copy-done | bytes 114712
  3.0 0.0 copy-start.2
  3.0 0.7 %copy-done.2 = s32[8,32,2]{1,2,0:T(2,128)S(1)} copy-done((s32[8,32,2]{1,2,0:T(2,128)S(1)}, s32[8,32,2]{1,2,0:T(2,128)}, u32[]{:S(2)}) %copy-start.2) | copy-done | bytes 2072
  3.7 0.0 copy-start.3
  3.7 0.7 %copy-done.3 = s32[8,32]{1,0:T(8,128)S(1)} copy-done((s32[8,32]{1,0:T(8,128)S(1)}, s32[8,32]{1,0:T(8,128)}, u32[]{:S(2)}) %copy-start.3) | copy-done | bytes 1048
  4.4 59.7 %shard_map.59 = (f32[4096,128]{1,0:T(8,128)S(1)}, f32[224,128]{1,0:T(8,128)S(1)}) custom-call(f32[3584,128]{1,0:T(8,128)S(1)} %bitcast.5, f32[224,128]{1,0:T(8,128)S(1)} %copy-done.1, s32[8,2,32]{2,1,0:T(2,128)S(1)} %bitcast.7, s32[8,32]{1,0:T(8,128)S(1)} %copy-done.3), custom_call_target="tpu_custom_call" | custom-call | tf_op jit(solution)/shard_map/pallas_call | solution.py:410
  64.1 1.3 %copy.8 = f32[2,128,16,128]{3,2,1,0:T(8,128)} copy(f32[2,128,16,128]{3,2,1,0:T(8,128)S(1)} %bitcast.4) | data formatting | bytes 4194304
  65.5 0.6 copy.9
Async XLA Ops:
  0.6 1.5 %copy-start = (f32[224,16,128]{2,1,0:T(8,128)S(1)}, f32[224,16,128]{2,1,0:T(8,128)}, u32[]{:S(2)}) copy-start(f32[224,16,128]{2,1,0:T(8,128)} %param.4) | copy-start | bytes 5505028
  2.1 0.9 %copy-start.1 = (f32[224,128]{1,0:T(8,128)S(1)}, f32[224,128]{1,0:T(8,128)}, u32[]{:S(2)}) copy-start(f32[224,128]{1,0:T(8,128)} %lib_hbm.1) | copy-start | bytes 344068
  3.0 0.7 %copy-start.2 = (s32[8,32,2]{1,2,0:T(2,128)S(1)}, s32[8,32,2]{1,2,0:T(2,128)}, u32[]{:S(2)}) copy-start(s32[8,32,2]{1,2,0:T(2,128)} %param.6) | copy-start | bytes 6148
  3.7 0.7 %copy-start.3 = (s32[8,32]{1,0:T(8,128)S(1)}, s32[8,32]{1,0:T(8,128)}, u32[]{:S(2)}) copy-start(s32[8,32]{1,0:T(8,128)} %counts_hbm.1) | copy-start | bytes 3076

commit v3 on v2

v3 whole, which is shorter than its diff:
```python
import functools

import jax
import jax.numpy as jnp
from jax import lax
from jax.experimental import pallas as pl
from jax.experimental.pallas import tpu as pltpu
from jax.sharding import PartitionSpec as P

MESH = pl.DeviceIdType.MESH
BANDS = 224
BLOCK = 128
SLOTS = 2
WIDE = SLOTS * BLOCK
TILE_H = 16
TILE_W = 128
PIX = TILE_H * TILE_W
PART = 32
SIZES = (32, 24)
CHIP = 56
ROWS = 8
COPIES = 8
VMEM_LIMIT = 60 * 1024 * 1024
YS = 4
PAIR = 2 * TILE_W
PAIRS = PIX // PAIR
STEP = 0.2
THRESHOLD = 0.05
F32 = jnp.float32
BF16 = jnp.bfloat16


def nn(a, b):
    return lax.dot_general(a, b, (((1,), (0,)), ((), ())), preferred_element_type=F32)


def nt(a, b):
    return lax.dot_general(a, b, (((1,), (1,)), ((), ())), preferred_element_type=F32)


def split(x):
    hi = x.astype(BF16)
    return hi, (x - hi.astype(F32)).astype(BF16)


def start_of(row):
    return row // 2 * CHIP + row % 2 * PART


def kernel(
    cols, pix_hbm, lib_hbm, ids_hbm, counts_hbm, abund_hbm, lgrad_hbm,
    pix, ids, counts, lhi, llo, gath, bsend, spec, a1, a2, a3, ones,
    rs, rr, hs, hr, gsend, grecv, gacc, gn, gy, gzs, gz, obuf, lgrad,
    send_z, recv_z, send_y, recv_y, send_b, recv_b, send_h, recv_h, send_g, recv_g,
    send_n, recv_n, send_ty, recv_ty, send_tz, recv_tz, send_c, recv_c, sem_in, sem_out,
):
    ny = YS
    nz = cols // ny
    r = lax.axis_index("row")
    c = lax.axis_index("col")
    z = c // ny
    y = lax.rem(c, ny)
    begin = pl.multiple_of(r // 2 * CHIP + lax.rem(r, 2) * PART, 8)

    def by_core(work):
        for k, size in enumerate(SIZES):
            pl.when(lax.rem(r, 2) == k)(functools.partial(work, size))

    def mine(size):
        return pl.ds(begin, size)

    near_first = sorted(range(1, nz), key=lambda d: (min(d, nz - d), d))

    def far(src, dst, ssem, rsem, dev):
        return pltpu.make_async_remote_copy(
            src_ref=src, dst_ref=dst, send_sem=ssem, recv_sem=rsem,
            device_id=dev, device_id_type=MESH,
        )

    def on_z(d):
        return (r, lax.rem(z + d, nz) * ny + y)

    def on_y(e):
        return (r, z * ny + lax.rem(y + e, ny))

    def on_row(k):
        return (lax.rem(r + k, ROWS), c)

    pix_in = pltpu.make_async_copy(pix_hbm, pix, sem_in.at[0])
    ids_in = pltpu.make_async_copy(ids_hbm, ids, sem_in.at[1])
    counts_in = pltpu.make_async_copy(counts_hbm, counts, sem_in.at[2])

    def lib_in(size):
        return pltpu.make_async_copy(
            lib_hbm.at[mine(size)], gath.at[y, 0, pl.ds(0, size)], sem_in.at[3]
        )

    by_core(lambda size: lib_in(size).start())
    ids_in.start()
    counts_in.start()
    pix_in.start()

    barrier = pltpu.get_barrier_semaphore()

    def greet(dev):
        pl.semaphore_signal(barrier, inc=1, device_id=dev, device_id_type=MESH)

    for d in range(1, nz):
        greet(on_z(d))
    for e in range(1, ny):
        greet(on_y(e))
    for k in range(1, ROWS):
        greet(on_row(k))

    @pl.when(c > 0)
    def _():
        greet((r, c - 1))

    @pl.when(c < cols - 1)
    def _():
        greet((r, c + 1))

    beside_cols = (c > 0).astype(jnp.int32) + (c < cols - 1).astype(jnp.int32)
    pl.semaphore_wait(barrier, nz - 1 + ny - 1 + ROWS - 1 + beside_cols)

    def lib_z(size, d):
        rows = pl.ds(0, size)
        return far(gath.at[y, 0, rows], gath.at[y, d, rows], send_z.at[d], recv_z.at[d], on_z(d))

    def lib_y(size, d, e):
        block = gath.at[y, d, pl.ds(0, size)]
        return far(block, block, send_y.at[d, e], recv_y.at[d, e], on_y(e))

    @by_core
    def _(size):
        lib_in(size).wait()
        for d in near_first:
            lib_z(size, d).start()
        for e in range(1, ny):
            lib_y(size, 0, e).start()

    lane = lax.broadcasted_iota(jnp.int32, (64, PIX), 1)
    which = lax.rem(lax.broadcasted_iota(jnp.int32, (64, PIX), 0), 32)
    spot = jnp.where(which < TILE_H, which * TILE_W, (which - TILE_H) * TILE_W + TILE_W - 1)
    ones[...] = jnp.where(lane == spot, 1.0, 0.0).astype(BF16)

    @pl.when(r == 0)
    def _():
        for i in range(2):
            rr[i, 0] = jnp.zeros((WIDE, TILE_W), F32)

    @pl.when(r == ROWS - 1)
    def _():
        for i in range(2):
            rr[i, 1] = jnp.zeros((WIDE, TILE_W), F32)

    @pl.when(c == 0)
    def _():
        for i in range(2):
            hr[i, :TILE_H] = jnp.zeros((TILE_H, WIDE), F32)

    @pl.when(c == cols - 1)
    def _():
        for i in range(2):
            hr[i, TILE_H:] = jnp.zeros((TILE_H, WIDE), F32)

    pix_in.wait()
    for h in range(TILE_H):
        hi, lo = split(pix[pl.ds(h, BANDS, TILE_H), :])
        lhi[WIDE:, h * TILE_W:(h + 1) * TILE_W] = hi
        llo[WIDE:, h * TILE_W:(h + 1) * TILE_W] = lo
    ids_in.wait()
    counts_in.wait()

    def choose(size, row, s):
        block = ids[row, s, c]
        use = jnp.where(counts[row, c] > s, 1.0, 0.0)
        return gath[lax.rem(block, ny), lax.rem(z - block // ny + nz, nz), :size] * use

    def spec_copy(size, k):
        return far(
            bsend.at[k, :, pl.ds(0, size)], spec.at[:, mine(size), :], send_b.at[k], recv_b.at[r], on_row(k)
        )

    @by_core
    def _(size):
        for d in near_first:
            lib_z(size, d).wait_recv()
            for e in range(1, ny):
                lib_y(size, d, e).start()
        for d in [0] + near_first:
            for e in range(1, ny):
                lib_y(size, d, e).wait_recv()
        for k in range(1, ROWS):
            for s in range(SLOTS):
                bsend[k, s, :size] = choose(size, lax.rem(r + k, ROWS), s)
            spec_copy(size, k).start()
        for s in range(SLOTS):
            spec[s, mine(size), :] = choose(size, r, s)

    for p in range(ROWS):
        @pl.when(r != p)
        def _():
            size = SIZES[p % 2]
            part = pl.ds(start_of(p), size)
            far(bsend.at[0, :, pl.ds(0, size)], spec.at[:, part, :], send_b.at[0], recv_b.at[p], (r, c)).wait_recv()

    spectra = jnp.concatenate([spec[0], spec[1]], axis=1)
    s_hi, s_lo = split(spectra)
    t_hi, t_lo = split(spectra.T)

    def lanes(j, pad=0):
        return slice(j * PAIR + pad, (j + 1) * PAIR + pad)

    def keep(j, value):
        hi, lo = split(value)
        lhi[:WIDE, lanes(j)] = hi
        llo[:WIDE, lanes(j)] = lo

    def row_copies(i):
        up = far(rs.at[i, 0], rr.at[i, 1], send_h.at[i, 2], recv_h.at[i, 3], (r - 1, c))
        down = far(rs.at[i, 1], rr.at[i, 0], send_h.at[i, 3], recv_h.at[i, 2], (r + 1, c))
        return up, down

    def col_copies(i):
        left = far(hs.at[i, :TILE_H], hr.at[i, TILE_H:], send_h.at[i, 0], recv_h.at[i, 1], (r, c - 1))
        right = far(hs.at[i, TILE_H:], hr.at[i, :TILE_H], send_h.at[i, 1], recv_h.at[i, 0], (r, c + 1))
        return left, right

    def act(low, high, pos, count, what):
        @pl.when(pos > 0)
        def _():
            if what == "start":
                low.start()
            elif what == "send":
                low.wait_send()
            else:
                high.wait_recv()

        @pl.when(pos < count - 1)
        def _():
            if what == "start":
                high.start()
            elif what == "send":
                high.wait_send()
            else:
                low.wait_recv()

    def edge_rows(i, what):
        act(*row_copies(i), r, ROWS, what)

    def edge_cols(i, what):
        act(*col_copies(i), c, cols, what)

    def pack(i):
        picked = ones[:32, :]
        hs[i] = nt(picked, lhi[:WIDE, :]) + nt(picked, llo[:WIDE, :])

    ends_first = [0, PAIRS - 1] + list(range(1, PAIRS - 1))

    for j in ends_first:
        p_hi = lhi[WIDE:, lanes(j)]
        p_lo = llo[WIDE:, lanes(j)]
        value = STEP * (nn(t_hi, p_hi) + nn(t_hi, p_lo) + nn(t_lo, p_hi))
        a1[:, lanes(j)] = value
        keep(j, value)
        if j == 0:
            rs[0, 0] = value[:, :TILE_W]
        if j == PAIRS - 1:
            rs[0, 1] = value[:, TILE_W:]
            edge_rows(0, "start")
    pack(0)
    edge_cols(0, "start")

    gram = nn(t_hi, s_hi) + nn(t_hi, s_lo) + nn(t_lo, s_hi)
    gi = lax.broadcasted_iota(jnp.int32, (WIDE, WIDE), 0)
    gj = lax.broadcasted_iota(jnp.int32, (WIDE, WIDE), 1)
    u_hi, u_lo = split(jnp.where(gi == gj, 0.4, 0.0) - STEP * gram)
    column = lax.broadcasted_iota(jnp.int32, (WIDE, TILE_W), 1)

    def beside(own):
        halves = []
        for q in range(2):
            x = own[:, q * TILE_W:(q + 1) * TILE_W]
            from_left = jnp.where(column == 0, 0.0, pltpu.roll(x, 1, 1))
            from_right = jnp.where(column == TILE_W - 1, 0.0, pltpu.roll(x, TILE_W - 1, 1))
            halves.append(from_left + from_right)
        return jnp.concatenate(halves, axis=1)

    def inner(j, own, excess):
        a_hi = lhi[:WIDE, lanes(j)]
        a_lo = llo[:WIDE, lanes(j)]
        value = nn(u_hi, a_hi) + nn(u_hi, a_lo) + nn(u_lo, a_hi)
        value = value + a1[:, lanes(j)] + STEP * (jnp.abs(excess) - THRESHOLD)
        return value + 0.1 * beside(own)

    def columns(i):
        hi, lo = split(hr[i])
        return jnp.concatenate([hi.astype(F32), lo.astype(F32)], axis=0).T.astype(BF16)

    def outer(i, j, side, a):
        if j == 0:
            above = jnp.concatenate([rr[i, 0], a[:, :TILE_W]], axis=1)
        else:
            above = a[:, lanes(j, -TILE_W)]
        if j == PAIRS - 1:
            below = jnp.concatenate([a[:, PIX - TILE_W:], rr[i, 1]], axis=1)
        else:
            below = a[:, lanes(j, TILE_W)]
        return 0.1 * (nn(side, ones[:, lanes(j)]) + above + below)

    for j in range(PAIRS):
        own = a1[:, lanes(j)]
        a2[:, lanes(j)] = inner(j, own, own - THRESHOLD)
    edge_rows(0, "recv")
    edge_cols(0, "recv")
    side1 = columns(0)
    for j in ends_first:
        value = a2[:, lanes(j)] + outer(0, j, side1, a1)
        a2[:, lanes(j)] = value
        keep(j, value)
        if j == 0:
            rs[1, 0] = value[:, :TILE_W]
        if j == PAIRS - 1:
            rs[1, 1] = value[:, TILE_W:]
            edge_rows(1, "start")
    pack(1)
    edge_cols(1, "start")
    for j in range(PAIRS):
        own = a2[:, lanes(j)]
        excess = own + jnp.minimum(a1[:, lanes(j)] - THRESHOLD, 0.0)
        a3[:, lanes(j)] = inner(j, own, excess)
    edge_rows(1, "recv")
    edge_cols(1, "recv")
    side2 = columns(1)
    for j in range(PAIRS):
        value = a3[:, lanes(j)] + outer(1, j, side2, a2)
        a3[:, lanes(j)] = value
        keep(j, value)

    both = (
        nt(lhi[...], lhi[:WIDE, :]) + nt(lhi[...], llo[:WIDE, :]) + nt(llo[...], lhi[:WIDE, :])
    )
    c_hi, c_lo = split(both[:WIDE])
    grad = nn(s_hi, c_hi) + nn(s_hi, c_lo) + nn(s_lo, c_hi) - both[WIDE:]
    for s in range(SLOTS):
        use = jnp.where(counts[r, c] > s, 1.0 / PIX, 0.0)
        gsend[s] = grad[:, s * BLOCK:(s + 1) * BLOCK] * use

    def grad_copy(p):
        size = SIZES[p % 2]
        return far(
            gsend.at[:, pl.ds(start_of(p), size), :], grecv.at[r, :, pl.ds(0, size)],
            send_g.at[p], recv_g.at[r], (p, c),
        )

    for p in range(ROWS):
        @pl.when(r != p)
        def _():
            grad_copy(p).start()

        @pl.when(r == p)
        def _():
            size = SIZES[p % 2]
            grecv[r, :, :size] = gsend[:, start_of(p):start_of(p) + size, :]

    for h in range(TILE_H):
        obuf[pl.ds(h, WIDE, TILE_H), :] = a3[:, h * TILE_W:(h + 1) * TILE_W]
    abund_out = pltpu.make_async_copy(obuf, abund_hbm, sem_out.at[0])
    abund_out.start()

    beside_z = [1, nz - 1] if nz > 3 else []
    far_first = [d for d in near_first[::-1] if d not in beside_z]

    def sum_n(size, i):
        rows = pl.ds(0, size)
        return far(
            gacc.at[:, beside_z[i], rows], gn.at[i, :, rows], send_n.at[i], recv_n.at[i], on_z(beside_z[i])
        )

    def sum_y(size, d, e):
        rows = pl.ds(0, size)
        return far(gacc.at[e, d, rows], gy.at[e, d, rows], send_ty.at[d, e], recv_ty.at[d, e], on_y(e))

    def sum_z(size, d):
        rows = pl.ds(0, size)
        return far(gzs.at[d, rows], gz.at[d, rows], send_tz.at[d], recv_tz.at[d], on_z(d))

    def part_copy(size, k):
        block = lgrad.at[mine(size)]
        return far(block, block, send_c.at[k], recv_c.at[r], on_row(k))

    @by_core
    def _(size):
        for q in range(ROWS):
            @pl.when(r != q)
            def _():
                far(
                    gsend.at[:, pl.ds(0, size), :], grecv.at[q, :, pl.ds(0, size)],
                    send_g.at[0], recv_g.at[q], (q, c),
                ).wait_recv()

        named = [[ids[q, s, c] for s in range(SLOTS)] for q in range(ROWS)]

        def collect(d, e):
            owner = lax.rem(z + d, nz) * ny + lax.rem(y + e, ny)
            total = jnp.zeros((size, BLOCK), F32)
            for q in range(ROWS):
                for s in range(SLOTS):
                    total = total + jnp.where(named[q][s] == owner, 1.0, 0.0) * grecv[q, s, :size]
            return total

        others = list(range(1, ny))
        for i, d in enumerate(beside_z):
            for e in range(ny):
                gacc[e, d, :size] = collect(d, e)
            sum_n(size, i).start()
        for d in far_first:
            for e in others + [0]:
                gacc[e, d, :size] = collect(d, e)
                if e:
                    sum_y(size, d, e).start()

        def forward(d):
            total = gacc[0, d, :size]
            for e in others:
                sum_y(size, d, e).wait_recv()
                total = total + gy[e, d, :size]
            if d:
                gzs[d, :size] = total
                sum_z(size, d).start()
            return total

        own = [collect(0, e) for e in range(ny)]
        for d in far_first[:1]:
            forward(d)
        for i in range(len(beside_z)):
            sum_n(size, i).wait_recv()
            own = [own[e] + gn[i, e, :size] for e in range(ny)]
        for e in others + [0]:
            gacc[e, 0, :size] = own[e]
            if e:
                sum_y(size, 0, e).start()
        for d in far_first[1:]:
            forward(d)
        total = forward(0)
        for d in far_first:
            sum_z(size, d).wait_recv()
            total = total + gz[d, :size]
        lgrad[mine(size), :] = total
        for k in range(1, ROWS):
            part_copy(size, k).start()

    for p in range(ROWS):
        @pl.when(r != p)
        def _():
            block = lgrad.at[pl.ds(start_of(p), SIZES[p % 2])]
            far(block, block, send_c.at[0], recv_c.at[p], (r, c)).wait_recv()

    lgrad_out = pltpu.make_async_copy(lgrad, lgrad_hbm, sem_out.at[1])
    lgrad_out.start()

    @by_core
    def _(size):
        for d in near_first:
            lib_z(size, d).wait_send()
        for d in range(nz):
            for e in range(1, ny):
                lib_y(size, d, e).wait_send()
        for i in range(len(beside_z)):
            sum_n(size, i).wait_send()
        for d in far_first:
            sum_z(size, d).wait_send()
        for d in far_first + [0]:
            for e in range(1, ny):
                sum_y(size, d, e).wait_send()
        for k in range(1, ROWS):
            spec_copy(size, k).wait_send()
            part_copy(size, k).wait_send()

    for p in range(ROWS):
        @pl.when(r != p)
        def _():
            grad_copy(p).wait_send()

    for i in range(2):
        edge_rows(i, "send")
        edge_cols(i, "send")
    abund_out.wait()
    lgrad_out.wait()


def finish(abund_in, lgrad_in, abund_out, lgrad_out, abund, lgrad, sems_in, sems_out):
    rows = abund_in.shape[0] // COPIES
    ways = [(lgrad_in, lgrad, lgrad_out)]
    for i in range(COPIES):
        part = pl.ds(i * rows, rows)
        ways.append((abund_in.at[part], abund.at[part], abund_out.at[part]))
    reads = [pltpu.make_async_copy(way[0], way[1], sems_in.at[i]) for i, way in enumerate(ways)]
    writes = [pltpu.make_async_copy(way[1], way[2], sems_out.at[i]) for i, way in enumerate(ways)]
    for read in reads:
        read.start()
    for read, write in zip(reads, writes):
        read.wait()
        write.start()
    for write in writes:
        write.wait()


def local(cols, pixels, library, block_ids, counts):
    dma = pltpu.SemaphoreType.DMA
    ny = YS
    nz = cols // ny
    hbm = pl.BlockSpec(memory_space=pltpu.HBM)
    shapes = (
        jax.ShapeDtypeStruct((WIDE * TILE_H, TILE_W), F32),
        jax.ShapeDtypeStruct((BANDS, BLOCK), F32),
    )
    abundance, grad = pl.pallas_call(
        functools.partial(kernel, cols),
        out_shape=shapes,
        in_specs=[hbm] * 4,
        out_specs=(hbm, hbm),
        scratch_shapes=[
            pltpu.VMEM((BANDS * TILE_H, TILE_W), F32),
            pltpu.SMEM((ROWS, SLOTS, cols), jnp.int32),
            pltpu.SMEM((ROWS, cols), jnp.int32),
            pltpu.VMEM((WIDE + BANDS, PIX), BF16),
            pltpu.VMEM((WIDE + BANDS, PIX), BF16),
            pltpu.VMEM((ny, nz, PART, BLOCK), F32),
            pltpu.VMEM((ROWS, SLOTS, PART, BLOCK), F32),
            pltpu.VMEM((SLOTS, BANDS, BLOCK), F32),
            pltpu.VMEM((WIDE, PIX), F32),
            pltpu.VMEM((WIDE, PIX), F32),
            pltpu.VMEM((WIDE, PIX), F32),
            pltpu.VMEM((64, PIX), BF16),
            pltpu.VMEM((2, 2, WIDE, TILE_W), F32),
            pltpu.VMEM((2, 2, WIDE, TILE_W), F32),
            pltpu.VMEM((2, 32, WIDE), F32),
            pltpu.VMEM((2, 32, WIDE), F32),
            pltpu.VMEM((SLOTS, BANDS, BLOCK), F32),
            pltpu.VMEM((ROWS, SLOTS, PART, BLOCK), F32),
            pltpu.VMEM((ny, nz, PART, BLOCK), F32),
            pltpu.VMEM((2, ny, PART, BLOCK), F32),
            pltpu.VMEM((ny, nz, PART, BLOCK), F32),
            pltpu.VMEM((nz, PART, BLOCK), F32),
            pltpu.VMEM((nz, PART, BLOCK), F32),
            pltpu.VMEM((WIDE * TILE_H, TILE_W), F32),
            pltpu.VMEM((BANDS, BLOCK), F32),
            dma((nz,)), dma((nz,)),
            dma((nz, ny)), dma((nz, ny)),
            dma((ROWS,)), dma((ROWS,)),
            dma((2, 4)), dma((2, 4)),
            dma((ROWS,)), dma((ROWS,)),
            dma((2,)), dma((2,)),
            dma((nz, ny)), dma((nz, ny)),
            dma((nz,)), dma((nz,)),
            dma((ROWS,)), dma((ROWS,)),
            dma((4,)), dma((2,)),
        ],
        compiler_params=pltpu.CompilerParams(
            collective_id=0, has_side_effects=True, vmem_limit_bytes=VMEM_LIMIT
        ),
    )(
        pixels.reshape(BANDS * TILE_H, TILE_W), library,
        block_ids.transpose(0, 2, 1), counts,
    )
    abundance, grad = pl.pallas_call(
        finish,
        out_shape=shapes,
        in_specs=[hbm, hbm],
        out_specs=(hbm, hbm),
        scratch_shapes=[
            pltpu.VMEM((WIDE * TILE_H, TILE_W), F32),
            pltpu.VMEM((BANDS, BLOCK), F32),
            dma((COPIES + 1,)), dma((COPIES + 1,)),
        ],
        compiler_params=pltpu.CompilerParams(vmem_limit_bytes=VMEM_LIMIT),
    )(abundance, grad)
    return abundance.reshape(SLOTS, BLOCK, TILE_H, TILE_W), grad.T


def solution(mesh):
    placed = (P(None, "row", "col"), P(None, "col"), P(), P())
    return jax.shard_map(
        functools.partial(local, mesh.shape["col"]),
        mesh=mesh,
        in_specs=placed,
        out_specs=(P(None, None, "row", "col"), P("col", None)),
        check_vma=False,
    )
```

time: 66.3 us -> 63 us (0.950)
  local copies, waits for them, and re-layouts: 5.74 us -> 0 us
  Pallas kernels: 59.7 us -> 62.2 us
    unnamed x10 -> x0, local copies, waits for them, and re-layouts: 5.74 us -> none
    pallas_call x1 -> x2, Pallas kernels: 59.7 us -> 62.2 us  [the longest x1 59.7 us: local(): pl.pallas_call(functools.partial(kernel, cols), out_shape=shapes, in_spec...]
where the time goes in v3:
time: 63 us; the launch traced here: 62.8 us
  Pallas kernels  62.2 us (99%)
  between operations  0.64 us (1%)
    pallas_call x1, Pallas kernels, local(): pl.pallas_call(functools.partial(kernel, cols), out_shape=shapes, in_spec...  59.7 us
    pallas_call x1, Pallas kernels, local(): pl.pallas_call(finish, out_shape=shapes, in_specs=[hbm, hbm], out_specs=(...  2.47 us

profile of v3, /device:TPU:1, one launch (start us, length us, event | category | flops | bytes accessed | tf_op | source)
XLA Modules:
  0.0 62.8 jit_solution(5670359776456006518)
XLA Ops:
  0.6 59.7 %shard_map.59 = (f32[4096,128]{1,0:T(8,128)}, f32[224,128]{1,0:T(8,128)}) custom-call(f32[3584,128]{1,0:T(8,128)} %bitcast.4, f32[224,128]{1,0:T(8,128)} %lib_hbm.1, s32[8,2,32]{2,1,0:T(2,128)} %bitcast.5, s32[8,32]{1,0:T(8,128)} %counts_hbm.1), custom_call_target="tpu_custom_call" | custom-call | tf_op jit(solution)/shard_map/pallas_call | solution.py:519
  60.4 2.5 %shard_map.60 = (f32[4096,128]{1,0:T(8,128)}, f32[224,128]{1,0:T(8,128)}) custom-call(f32[4096,128]{1,0:T(8,128)} %get-tuple-element.6.abund_in, f32[224,128]{1,0:T(8,128)} %get-tuple-element.7.lgrad_in), custom_call_target="tpu_custom_call" | custom-call | tf_op jit(solution)/shard_map/pallas_call | solution.py:568

commit v4 on v3

--- a/solution.py
+++ b/solution.py
@@ -50,8 +50,8 @@
 def kernel(
     cols, pix_hbm, lib_hbm, ids_hbm, counts_hbm, abund_hbm, lgrad_hbm,
     pix, ids, counts, lhi, llo, gath, bsend, spec, a1, a2, a3, ones,
-    rs, rr, hs, hr, gsend, grecv, gacc, gn, gy, gzs, gz, obuf, lgrad,
-    send_z, recv_z, send_y, recv_y, send_b, recv_b, send_h, recv_h, send_g, recv_g,
+    rs, rr, hs, hr, cs, cr, gsend, grecv, gacc, gn, gy, gzs, gz, obuf, lgrad,
+    send_z, recv_z, send_y, recv_y, send_b, recv_b, send_h, recv_h, send_k, recv_k, send_g, recv_g,
     send_n, recv_n, send_ty, recv_ty, send_tz, recv_tz, send_c, recv_c, sem_in, sem_out,
 ):
     ny = YS
@@ -120,8 +120,21 @@
     def _():
         greet((r, c + 1))
 
+    corners = ((-1, -1, 0, 3), (1, -1, TILE_H - 1, 2), (-1, 1, TILE_H, 1), (1, 1, 2 * TILE_H - 1, 0))
+
+    def within(dr, dc):
+        return (r + dr >= 0) & (r + dr < ROWS) & (c + dc >= 0) & (c + dc < cols)
+
+    across = jnp.int32(0)
+    for dr, dc, _, _ in corners:
+        across = across + within(dr, dc).astype(jnp.int32)
+
+        @pl.when(within(dr, dc))
+        def _():
+            greet((r + dr, c + dc))
+
     beside_cols = (c > 0).astype(jnp.int32) + (c < cols - 1).astype(jnp.int32)
-    pl.semaphore_wait(barrier, nz - 1 + ny - 1 + ROWS - 1 + beside_cols)
+    pl.semaphore_wait(barrier, nz - 1 + ny - 1 + ROWS - 1 + beside_cols + across)
 
     def lib_z(size, d):
         rows = pl.ds(0, size)
@@ -163,6 +176,11 @@
     def _():
         for i in range(2):
             hr[i, TILE_H:] = jnp.zeros((TILE_H, WIDE), F32)
+
+    for dr, dc, _, place in corners:
+        @pl.when(jnp.logical_not(within(dr, dc)))
+        def _():
+            cr[3 - place] = jnp.zeros((8, WIDE), F32)
 
     pix_in.wait()
     for h in range(TILE_H):
@@ -258,6 +276,22 @@
 
     ends_first = [0, PAIRS - 1] + list(range(1, PAIRS - 1))
 
+    def corner_copy(i):
+        dr, dc, _, place = corners[i]
+        return far(cs.at[i], cr.at[place], send_k.at[i], recv_k.at[place], (r + dr, c + dc))
+
+    def edge_corners(what):
+        for i, (dr, dc, row, place) in enumerate(corners):
+            @pl.when(within(dr, dc))
+            def _():
+                if what == "start":
+                    cs[i] = jnp.broadcast_to(hs[0, row:row + 1, :], (8, WIDE))
+                    corner_copy(i).start()
+                elif what == "send":
+                    corner_copy(i).wait_send()
+                else:
+                    corner_copy(3 - i).wait_recv()
+
     for j in ends_first:
         p_hi = lhi[WIDE:, lanes(j)]
         p_lo = llo[WIDE:, lanes(j)]
@@ -271,6 +305,7 @@
             edge_rows(0, "start")
     pack(0)
     edge_cols(0, "start")
+    edge_corners("start")
 
     gram = nn(t_hi, s_hi) + nn(t_hi, s_lo) + nn(t_lo, s_hi)
     gi = lax.broadcasted_iota(jnp.int32, (WIDE, WIDE), 0)
@@ -287,36 +322,38 @@
             halves.append(from_left + from_right)
         return jnp.concatenate(halves, axis=1)
 
-    def inner(j, own, excess):
+    blank = jnp.zeros((WIDE, TILE_W), F32)
+
+    def inner(j, a, excess):
+        own = a[:, lanes(j)]
         a_hi = lhi[:WIDE, lanes(j)]
         a_lo = llo[:WIDE, lanes(j)]
         value = nn(u_hi, a_hi) + nn(u_hi, a_lo) + nn(u_lo, a_hi)
         value = value + a1[:, lanes(j)] + STEP * (jnp.abs(excess) - THRESHOLD)
-        return value + 0.1 * beside(own)
-
-    def columns(i):
-        hi, lo = split(hr[i])
-        return jnp.concatenate([hi.astype(F32), lo.astype(F32)], axis=0).T.astype(BF16)
-
-    def outer(i, j, side, a):
         if j == 0:
-            above = jnp.concatenate([rr[i, 0], a[:, :TILE_W]], axis=1)
+            above = jnp.concatenate([blank, a[:, :TILE_W]], axis=1)
         else:
             above = a[:, lanes(j, -TILE_W)]
         if j == PAIRS - 1:
-            below = jnp.concatenate([a[:, PIX - TILE_W:], rr[i, 1]], axis=1)
+            below = jnp.concatenate([a[:, PIX - TILE_W:], blank], axis=1)
         else:
             below = a[:, lanes(j, TILE_W)]
-        return 0.1 * (nn(side, ones[:, lanes(j)]) + above + below)
-
-    for j in range(PAIRS):
-        own = a1[:, lanes(j)]
-        a2[:, lanes(j)] = inner(j, own, own - THRESHOLD)
-    edge_rows(0, "recv")
-    edge_cols(0, "recv")
-    side1 = columns(0)
+        return value + 0.1 * (beside(own) + above + below)
+
+    def columns(edge):
+        hi, lo = split(edge)
+        return jnp.concatenate([hi.astype(F32), lo.astype(F32)], axis=0).T.astype(BF16)
+
+    def outer(j, side, above, below):
+        value = nn(side, ones[:, lanes(j)])
+        if j == 0:
+            value = value + jnp.concatenate([above, blank], axis=1)
+        if j == PAIRS - 1:
+            value = value + jnp.concatenate([blank, below], axis=1)
+        return 0.1 * value
+
     for j in ends_first:
-        value = a2[:, lanes(j)] + outer(0, j, side1, a1)
+        value = inner(j, a1, a1[:, lanes(j)] - THRESHOLD)
         a2[:, lanes(j)] = value
         keep(j, value)
         if j == 0:
@@ -326,15 +363,30 @@
             edge_rows(1, "start")
     pack(1)
     edge_cols(1, "start")
+    edge_rows(0, "recv")
+    edge_cols(0, "recv")
+    side1 = columns(hr[0])
     for j in range(PAIRS):
-        own = a2[:, lanes(j)]
-        excess = own + jnp.minimum(a1[:, lanes(j)] - THRESHOLD, 0.0)
-        a3[:, lanes(j)] = inner(j, own, excess)
+        value = a2[:, lanes(j)] + outer(j, side1, rr[0, 0], rr[0, 1])
+        a2[:, lanes(j)] = value
+        keep(j, value)
+    for j in range(PAIRS):
+        excess = a2[:, lanes(j)] + jnp.minimum(a1[:, lanes(j)] - THRESHOLD, 0.0)
+        a3[:, lanes(j)] = inner(j, a2, excess)
     edge_rows(1, "recv")
     edge_cols(1, "recv")
-    side2 = columns(1)
+    edge_corners("recv")
+
+    above2 = rr[1, 0] + jnp.where(r > 0, 0.1, 0.0) * a1[:, :TILE_W]
+    below2 = rr[1, 1] + jnp.where(r < ROWS - 1, 0.1, 0.0) * a1[:, PIX - TILE_W:]
+    row = lax.broadcasted_iota(jnp.int32, (2 * TILE_H, WIDE), 0)
+    share = jnp.where(row < TILE_H, jnp.where(c > 0, 0.1, 0.0), jnp.where(c < cols - 1, 0.1, 0.0))
+    edge2 = hr[1] + share * hs[0]
+    for place, at in enumerate((0, TILE_H - 1, TILE_H, 2 * TILE_H - 1)):
+        edge2 = edge2 + jnp.where(row == at, 0.2 * cr[place, :1, :], 0.0)
+    side2 = columns(edge2)
     for j in range(PAIRS):
-        value = a3[:, lanes(j)] + outer(1, j, side2, a2)
+        value = a3[:, lanes(j)] + outer(j, side2, above2, below2)
         a3[:, lanes(j)] = value
         keep(j, value)
 
@@ -486,6 +538,7 @@
     for i in range(2):
         edge_rows(i, "send")
         edge_cols(i, "send")
+    edge_corners("send")
     abund_out.wait()
     lgrad_out.wait()
 
@@ -538,6 +591,8 @@
             pltpu.VMEM((2, 2, WIDE, TILE_W), F32),
             pltpu.VMEM((2, 32, WIDE), F32),
             pltpu.VMEM((2, 32, WIDE), F32),
+            pltpu.VMEM((4, 8, WIDE), F32),
+            pltpu.VMEM((4, 8, WIDE), F32),
             pltpu.VMEM((SLOTS, BANDS, BLOCK), F32),
             pltpu.VMEM((ROWS, SLOTS, PART, BLOCK), F32),
             pltpu.VMEM((ny, nz, PART, BLOCK), F32),
@@ -551,6 +606,7 @@
             dma((nz, ny)), dma((nz, ny)),
             dma((ROWS,)), dma((ROWS,)),
             dma((2, 4)), dma((2, 4)),
+            dma((4,)), dma((4,)),
             dma((ROWS,)), dma((ROWS,)),
             dma((2,)), dma((2,)),
             dma((nz, ny)), dma((nz, ny)),

time: 63 us -> 60.8 us (0.965)
  Pallas kernels: 62.2 us -> 60.1 us
    pallas_call x1, Pallas kernels: 59.7 us -> 57.6 us  [local(): pl.pallas_call(functools.partial(kernel, cols), out_shape=shapes, in_spec...]
where the time goes in v4:
time: 60.8 us; the launch traced here: 60.7 us
  Pallas kernels  60.1 us (99%)
  between operations  0.64 us (1%)
    pallas_call x1, Pallas kernels, local(): pl.pallas_call(functools.partial(kernel, cols), out_shape=shapes, in_spec...  57.6 us
    pallas_call x1, Pallas kernels, local(): pl.pallas_call(finish, out_shape=shapes, in_specs=[hbm, hbm], out_specs=(...  2.47 us

profile of v4, /device:TPU:1, one launch (start us, length us, event | category | flops | bytes accessed | tf_op | source)
XLA Modules:
  0.0 60.7 jit_solution(4234520588032993537)
XLA Ops:
  0.6 57.6 %shard_map.59 = (f32[4096,128]{1,0:T(8,128)}, f32[224,128]{1,0:T(8,128)}) custom-call(f32[3584,128]{1,0:T(8,128)} %bitcast.4, f32[224,128]{1,0:T(8,128)} %lib_hbm.1, s32[8,2,32]{2,1,0:T(2,128)} %bitcast.5, s32[8,32]{1,0:T(8,128)} %counts_hbm.1), custom_call_target="tpu_custom_call" | custom-call | tf_op jit(solution)/shard_map/pallas_call | solution.py:572
  58.2 2.5 %shard_map.60 = (f32[4096,128]{1,0:T(8,128)}, f32[224,128]{1,0:T(8,128)}) custom-call(f32[4096,128]{1,0:T(8,128)} %get-tuple-element.6.abund_in, f32[224,128]{1,0:T(8,128)} %get-tuple-element.7.lgrad_in), custom_call_target="tpu_custom_call" | custom-call | tf_op jit(solution)/shard_map/pallas_call | solution.py:624

commit v5 on v4

--- a/solution.py
+++ b/solution.py
@@ -19,7 +19,8 @@
 SIZES = (32, 24)
 CHIP = 56
 ROWS = 8
-COPIES = 8
+COPIES = 4
+ROW_ORDER = (4, 3, 5, 2, 6, 1, 7)
 VMEM_LIMIT = 60 * 1024 * 1024
 YS = 4
 PAIR = 2 * TILE_W
@@ -105,12 +106,12 @@
     def greet(dev):
         pl.semaphore_signal(barrier, inc=1, device_id=dev, device_id_type=MESH)
 
-    for d in range(1, nz):
+    for d in near_first[::-1]:
         greet(on_z(d))
+    for k in ROW_ORDER:
+        greet(on_row(k))
     for e in range(1, ny):
         greet(on_y(e))
-    for k in range(1, ROWS):
-        greet(on_row(k))
 
     @pl.when(c > 0)
     def _():
@@ -209,7 +210,7 @@
         for d in [0] + near_first:
             for e in range(1, ny):
                 lib_y(size, d, e).wait_recv()
-        for k in range(1, ROWS):
+        for k in ROW_ORDER:
             for s in range(SLOTS):
                 bsend[k, s, :size] = choose(size, lax.rem(r + k, ROWS), s)
             spec_copy(size, k).start()
@@ -399,22 +400,20 @@
         use = jnp.where(counts[r, c] > s, 1.0 / PIX, 0.0)
         gsend[s] = grad[:, s * BLOCK:(s + 1) * BLOCK] * use
 
-    def grad_copy(p):
-        size = SIZES[p % 2]
+    def grad_copy(size, k):
+        other = SIZES[(SIZES.index(size) + k) % 2]
+        row, _ = on_row(k)
+        first = pl.multiple_of(row // 2 * CHIP + lax.rem(row, 2) * PART, 8)
         return far(
-            gsend.at[:, pl.ds(start_of(p), size), :], grecv.at[r, :, pl.ds(0, size)],
-            send_g.at[p], recv_g.at[r], (p, c),
+            gsend.at[:, pl.ds(first, other), :], grecv.at[r, :, pl.ds(0, other)],
+            send_g.at[k], recv_g.at[r], on_row(k),
         )
 
-    for p in range(ROWS):
-        @pl.when(r != p)
-        def _():
-            grad_copy(p).start()
-
-        @pl.when(r == p)
-        def _():
-            size = SIZES[p % 2]
-            grecv[r, :, :size] = gsend[:, start_of(p):start_of(p) + size, :]
+    @by_core
+    def _(size):
+        for k in ROW_ORDER:
+            grad_copy(size, k).start()
+        grecv[r, :, :size] = gsend[:, mine(size), :]
 
     for h in range(TILE_H):
         obuf[pl.ds(h, WIDE, TILE_H), :] = a3[:, h * TILE_W:(h + 1) * TILE_W]
@@ -439,8 +438,12 @@
         return far(gzs.at[d, rows], gz.at[d, rows], send_tz.at[d], recv_tz.at[d], on_z(d))
 
     def part_copy(size, k):
-        block = lgrad.at[mine(size)]
-        return far(block, block, send_c.at[k], recv_c.at[r], on_row(k))
+        return far(
+            lgrad.at[mine(size)], lgrad_hbm.at[mine(size)], send_c.at[k], recv_c.at[r], on_row(k)
+        )
+
+    def part_out(size):
+        return pltpu.make_async_copy(lgrad.at[mine(size)], lgrad_hbm.at[mine(size)], sem_out.at[1])
 
     @by_core
     def _(size):
@@ -500,20 +503,10 @@
             sum_z(size, d).wait_recv()
             total = total + gz[d, :size]
         lgrad[mine(size), :] = total
-        for k in range(1, ROWS):
+        for k in ROW_ORDER:
             part_copy(size, k).start()
-
-    for p in range(ROWS):
-        @pl.when(r != p)
-        def _():
-            block = lgrad.at[pl.ds(start_of(p), SIZES[p % 2])]
-            far(block, block, send_c.at[0], recv_c.at[p], (r, c)).wait_recv()
-
-    lgrad_out = pltpu.make_async_copy(lgrad, lgrad_hbm, sem_out.at[1])
-    lgrad_out.start()
-
-    @by_core
-    def _(size):
+        part_out(size).start()
+
         for d in near_first:
             lib_z(size, d).wait_send()
         for d in range(nz):
@@ -526,21 +519,27 @@
         for d in far_first + [0]:
             for e in range(1, ny):
                 sum_y(size, d, e).wait_send()
-        for k in range(1, ROWS):
+        for k in ROW_ORDER:
             spec_copy(size, k).wait_send()
-            part_copy(size, k).wait_send()
-
-    for p in range(ROWS):
-        @pl.when(r != p)
-        def _():
-            grad_copy(p).wait_send()
+            grad_copy(size, k).wait_send()
 
     for i in range(2):
         edge_rows(i, "send")
         edge_cols(i, "send")
     edge_corners("send")
     abund_out.wait()
-    lgrad_out.wait()
+
+    for p in range(ROWS):
+        @pl.when(r != p)
+        def _():
+            part = pl.ds(start_of(p), SIZES[p % 2])
+            far(lgrad.at[part], lgrad_hbm.at[part], send_c.at[0], recv_c.at[p], (r, c)).wait_recv()
+
+    @by_core
+    def _(size):
+        part_out(size).wait()
+        for k in ROW_ORDER:
+            part_copy(size, k).wait_send()
 
 
 def finish(abund_in, lgrad_in, abund_out, lgrad_out, abund, lgrad, sems_in, sems_out):

time: 60.8 us -> 59.2 us (0.974)
  Pallas kernels: 60.1 us -> 58.4 us
    pallas_call x1, Pallas kernels: 57.6 us -> 55.9 us  [local(): pl.pallas_call(functools.partial(kernel, cols), out_shape=shapes, in_spec...]
where the time goes in v5:
time: 59.2 us; the launch traced here: 59.1 us
  Pallas kernels  58.4 us (99%)
  between operations  0.64 us (1%)
    pallas_call x1, Pallas kernels, local(): pl.pallas_call(functools.partial(kernel, cols), out_shape=shapes, in_spec...  55.9 us
    pallas_call x1, Pallas kernels, local(): pl.pallas_call(finish, out_shape=shapes, in_specs=[hbm, hbm], out_specs=(...  2.5 us

profile of v5, /device:TPU:1, one launch (start us, length us, event | category | flops | bytes accessed | tf_op | source)
XLA Modules:
  0.0 59.1 jit_solution(8235916083094819882)
XLA Ops:
  0.6 55.9 %shard_map.59 = (f32[4096,128]{1,0:T(8,128)}, f32[224,128]{1,0:T(8,128)}) custom-call(f32[3584,128]{1,0:T(8,128)} %bitcast.4, f32[224,128]{1,0:T(8,128)} %lib_hbm.1, s32[8,2,32]{2,1,0:T(2,128)} %bitcast.5, s32[8,32]{1,0:T(8,128)} %counts_hbm.1), custom_call_target="tpu_custom_call" | custom-call | tf_op jit(solution)/shard_map/pallas_call | solution.py:571
  56.6 2.5 %shard_map.60 = (f32[4096,128]{1,0:T(8,128)}, f32[224,128]{1,0:T(8,128)}) custom-call(f32[4096,128]{1,0:T(8,128)} %get-tuple-element.6.abund_in, f32[224,128]{1,0:T(8,128)} %get-tuple-element.7.lgrad_in), custom_call_target="tpu_custom_call" | custom-call | tf_op jit(solution)/shard_map/pallas_call | solution.py:623

commit v6 on v5

--- a/solution.py
+++ b/solution.py
@@ -71,6 +71,11 @@
         return pl.ds(begin, size)
 
     near_first = sorted(range(1, nz), key=lambda d: (min(d, nz - d), d))
+    place = {d: i for i, d in enumerate([0] + near_first)}
+    rings = [[0]] + [[d for d in near_first if min(d, nz - d) == g] for g in range(1, nz // 2 + 1)]
+
+    def span(g):
+        return pl.ds(place[rings[g][0]], len(rings[g]))
 
     def far(src, dst, ssem, rsem, dev):
         return pltpu.make_async_remote_copy(
@@ -139,11 +144,11 @@
 
     def lib_z(size, d):
         rows = pl.ds(0, size)
-        return far(gath.at[y, 0, rows], gath.at[y, d, rows], send_z.at[d], recv_z.at[d], on_z(d))
-
-    def lib_y(size, d, e):
-        block = gath.at[y, d, pl.ds(0, size)]
-        return far(block, block, send_y.at[d, e], recv_y.at[d, e], on_y(e))
+        return far(gath.at[y, 0, rows], gath.at[y, place[d], rows], send_z.at[d], recv_z.at[d], on_z(d))
+
+    def lib_y(size, g, e):
+        block = gath.at[y, span(g), pl.ds(0, size)]
+        return far(block, block, send_y.at[g, e], recv_y.at[g, e], on_y(e))
 
     @by_core
     def _(size):
@@ -178,10 +183,10 @@
         for i in range(2):
             hr[i, TILE_H:] = jnp.zeros((TILE_H, WIDE), F32)
 
-    for dr, dc, _, place in corners:
+    for dr, dc, _, spot_at in corners:
         @pl.when(jnp.logical_not(within(dr, dc)))
         def _():
-            cr[3 - place] = jnp.zeros((8, WIDE), F32)
+            cr[3 - spot_at] = jnp.zeros((8, WIDE), F32)
 
     pix_in.wait()
     for h in range(TILE_H):
@@ -194,7 +199,9 @@
     def choose(size, row, s):
         block = ids[row, s, c]
         use = jnp.where(counts[row, c] > s, 1.0, 0.0)
-        return gath[lax.rem(block, ny), lax.rem(z - block // ny + nz, nz), :size] * use
+        d = lax.rem(z - block // ny + nz, nz)
+        at = jnp.where(d <= nz // 2, jnp.maximum(2 * d - 1, 0), 2 * (nz - d))
+        return gath[lax.rem(block, ny), at, :size] * use
 
     def spec_copy(size, k):
         return far(
@@ -203,13 +210,14 @@
 
     @by_core
     def _(size):
-        for d in near_first:
-            lib_z(size, d).wait_recv()
+        for g in range(1, len(rings)):
+            for d in rings[g]:
+                lib_z(size, d).wait_recv()
+            for e in sorted(range(1, ny), key=lambda e: -min(e, ny - e)):
+                lib_y(size, g, e).start()
+        for g in range(len(rings)):
             for e in range(1, ny):
-                lib_y(size, d, e).start()
-        for d in [0] + near_first:
-            for e in range(1, ny):
-                lib_y(size, d, e).wait_recv()
+                lib_y(size, g, e).wait_recv()
         for k in ROW_ORDER:
             for s in range(SLOTS):
                 bsend[k, s, :size] = choose(size, lax.rem(r + k, ROWS), s)
@@ -275,14 +283,12 @@
         picked = ones[:32, :]
         hs[i] = nt(picked, lhi[:WIDE, :]) + nt(picked, llo[:WIDE, :])
 
-    ends_first = [0, PAIRS - 1] + list(range(1, PAIRS - 1))
-
     def corner_copy(i):
-        dr, dc, _, place = corners[i]
-        return far(cs.at[i], cr.at[place], send_k.at[i], recv_k.at[place], (r + dr, c + dc))
+        dr, dc, _, spot_at = corners[i]
+        return far(cs.at[i], cr.at[spot_at], send_k.at[i], recv_k.at[spot_at], (r + dr, c + dc))
 
     def edge_corners(what):
-        for i, (dr, dc, row, place) in enumerate(corners):
+        for i, (dr, dc, row, _) in enumerate(corners):
             @pl.when(within(dr, dc))
             def _():
                 if what == "start":
@@ -293,20 +299,21 @@
                 else:
                     corner_copy(3 - i).wait_recv()
 
-    for j in ends_first:
+    def first(j):
         p_hi = lhi[WIDE:, lanes(j)]
         p_lo = llo[WIDE:, lanes(j)]
         value = STEP * (nn(t_hi, p_hi) + nn(t_hi, p_lo) + nn(t_lo, p_hi))
         a1[:, lanes(j)] = value
         keep(j, value)
-        if j == 0:
-            rs[0, 0] = value[:, :TILE_W]
-        if j == PAIRS - 1:
-            rs[0, 1] = value[:, TILE_W:]
-            edge_rows(0, "start")
-    pack(0)
-    edge_cols(0, "start")
-    edge_corners("start")
+        return value
+
+    rim = [0, PAIRS - 1]
+    rs[0, 0] = first(0)[:, :TILE_W]
+    rs[0, 1] = first(PAIRS - 1)[:, TILE_W:]
+    edge_rows(0, "start")
+    for j in (1, PAIRS - 2):
+        first(j)
+
 
     gram = nn(t_hi, s_hi) + nn(t_hi, s_lo) + nn(t_lo, s_hi)
     gi = lax.broadcasted_iota(jnp.int32, (WIDE, WIDE), 0)
@@ -353,15 +360,23 @@
             value = value + jnp.concatenate([blank, below], axis=1)
         return 0.1 * value
 
-    for j in ends_first:
+    def second(j):
         value = inner(j, a1, a1[:, lanes(j)] - THRESHOLD)
         a2[:, lanes(j)] = value
-        keep(j, value)
-        if j == 0:
-            rs[1, 0] = value[:, :TILE_W]
-        if j == PAIRS - 1:
-            rs[1, 1] = value[:, TILE_W:]
-            edge_rows(1, "start")
+        return value
+
+    rs[1, 0] = second(0)[:, :TILE_W]
+    rs[1, 1] = second(PAIRS - 1)[:, TILE_W:]
+    edge_rows(1, "start")
+    for j in range(2, PAIRS - 2):
+        first(j)
+    pack(0)
+    edge_cols(0, "start")
+    edge_corners("start")
+    for j in range(1, PAIRS - 1):
+        keep(j, second(j))
+    for j in rim:
+        keep(j, a2[:, lanes(j)])
     pack(1)
     edge_cols(1, "start")
     edge_rows(0, "recv")
@@ -383,8 +398,8 @@
     row = lax.broadcasted_iota(jnp.int32, (2 * TILE_H, WIDE), 0)
     share = jnp.where(row < TILE_H, jnp.where(c > 0, 0.1, 0.0), jnp.where(c < cols - 1, 0.1, 0.0))
     edge2 = hr[1] + share * hs[0]
-    for place, at in enumerate((0, TILE_H - 1, TILE_H, 2 * TILE_H - 1)):
-        edge2 = edge2 + jnp.where(row == at, 0.2 * cr[place, :1, :], 0.0)
+    for spot_at, at in enumerate((0, TILE_H - 1, TILE_H, 2 * TILE_H - 1)):
+        edge2 = edge2 + jnp.where(row == at, 0.2 * cr[spot_at, :1, :], 0.0)
     side2 = columns(edge2)
     for j in range(PAIRS):
         value = a3[:, lanes(j)] + outer(j, side2, above2, below2)
@@ -421,17 +436,20 @@
     abund_out.start()
 
     beside_z = [1, nz - 1] if nz > 3 else []
-    far_first = [d for d in near_first[::-1] if d not in beside_z]
+    far_rings = [g for g in range(len(rings) - 1, 0, -1) if rings[g] != beside_z]
+    far_first = [d for g in far_rings for d in rings[g]]
 
     def sum_n(size, i):
         rows = pl.ds(0, size)
         return far(
-            gacc.at[:, beside_z[i], rows], gn.at[i, :, rows], send_n.at[i], recv_n.at[i], on_z(beside_z[i])
+            gacc.at[:, place[beside_z[i]], rows], gn.at[i, :, rows], send_n.at[i], recv_n.at[i], on_z(beside_z[i])
         )
 
-    def sum_y(size, d, e):
+    def sum_y(size, g, e):
         rows = pl.ds(0, size)
-        return far(gacc.at[e, d, rows], gy.at[e, d, rows], send_ty.at[d, e], recv_ty.at[d, e], on_y(e))
+        return far(
+            gacc.at[e, span(g), rows], gy.at[e, span(g), rows], send_ty.at[g, e], recv_ty.at[g, e], on_y(e)
+        )
 
     def sum_z(size, d):
         rows = pl.ds(0, size)
@@ -465,30 +483,33 @@
                     total = total + jnp.where(named[q][s] == owner, 1.0, 0.0) * grecv[q, s, :size]
             return total
 
-        others = list(range(1, ny))
+        others = sorted(range(1, ny), key=lambda e: -min(e, ny - e))
         for i, d in enumerate(beside_z):
             for e in range(ny):
-                gacc[e, d, :size] = collect(d, e)
+                gacc[e, place[d], :size] = collect(d, e)
             sum_n(size, i).start()
-        for d in far_first:
+        for g in far_rings:
             for e in others + [0]:
-                gacc[e, d, :size] = collect(d, e)
+                for d in rings[g]:
+                    gacc[e, place[d], :size] = collect(d, e)
                 if e:
-                    sum_y(size, d, e).start()
-
-        def forward(d):
-            total = gacc[0, d, :size]
+                    sum_y(size, g, e).start()
+
+        def forward(g):
             for e in others:
-                sum_y(size, d, e).wait_recv()
-                total = total + gy[e, d, :size]
-            if d:
-                gzs[d, :size] = total
-                sum_z(size, d).start()
+                sum_y(size, g, e).wait_recv()
+            for d in rings[g]:
+                total = gacc[0, place[d], :size]
+                for e in others:
+                    total = total + gy[e, place[d], :size]
+                if d:
+                    gzs[d, :size] = total
+                    sum_z(size, d).start()
             return total
 
         own = [collect(0, e) for e in range(ny)]
-        for d in far_first[:1]:
-            forward(d)
+        for g in far_rings[:1]:
+            forward(g)
         for i in range(len(beside_z)):
             sum_n(size, i).wait_recv()
             own = [own[e] + gn[i, e, :size] for e in range(ny)]
@@ -496,8 +517,8 @@
             gacc[e, 0, :size] = own[e]
             if e:
                 sum_y(size, 0, e).start()
-        for d in far_first[1:]:
-            forward(d)
+        for g in far_rings[1:]:
+            forward(g)
         total = forward(0)
         for d in far_first:
             sum_z(size, d).wait_recv()
@@ -509,16 +530,16 @@
 
         for d in near_first:
             lib_z(size, d).wait_send()
-        for d in range(nz):
+        for g in range(len(rings)):
             for e in range(1, ny):
-                lib_y(size, d, e).wait_send()
+                lib_y(size, g, e).wait_send()
         for i in range(len(beside_z)):
             sum_n(size, i).wait_send()
         for d in far_first:
             sum_z(size, d).wait_send()
-        for d in far_first + [0]:
+        for g in far_rings + [0]:
             for e in range(1, ny):
-                sum_y(size, d, e).wait_send()
+                sum_y(size, g, e).wait_send()
         for k in ROW_ORDER:
             spec_copy(size, k).wait_send()
             grad_copy(size, k).wait_send()

time: 59.2 us -> 58.7 us (level)
  no operation moved by 1% of the time
where the time goes in v6:
time: 58.7 us; the launch traced here: 58.6 us
  Pallas kernels  57.9 us (99%)
  between operations  0.64 us (1%)
    pallas_call x1, Pallas kernels, local(): pl.pallas_call(functools.partial(kernel, cols), out_shape=shapes, in_spec...  55.4 us
    pallas_call x1, Pallas kernels, local(): pl.pallas_call(finish, out_shape=shapes, in_specs=[hbm, hbm], out_specs=(...  2.5 us

profile of v6, /device:TPU:1, one launch (start us, length us, event | category | flops | bytes accessed | tf_op | source)
XLA Modules:
  0.0 58.6 jit_solution(5877180628935924091)
XLA Ops:
  0.6 55.4 %shard_map.59 = (f32[4096,128]{1,0:T(8,128)}, f32[224,128]{1,0:T(8,128)}) custom-call(f32[3584,128]{1,0:T(8,128)} %bitcast.4, f32[224,128]{1,0:T(8,128)} %lib_hbm.1, s32[8,2,32]{2,1,0:T(2,128)} %bitcast.5, s32[8,32]{1,0:T(8,128)} %counts_hbm.1), custom_call_target="tpu_custom_call" | custom-call | tf_op jit(solution)/shard_map/pallas_call | solution.py:592
  56.1 2.5 %shard_map.60 = (f32[4096,128]{1,0:T(8,128)}, f32[224,128]{1,0:T(8,128)}) custom-call(f32[4096,128]{1,0:T(8,128)} %get-tuple-element.6.abund_in, f32[224,128]{1,0:T(8,128)} %get-tuple-element.7.lgrad_in), custom_call_target="tpu_custom_call" | custom-call | tf_op jit(solution)/shard_map/pallas_call | solution.py:644

commit v7 on v6

--- a/solution.py
+++ b/solution.py
@@ -118,11 +118,14 @@
     for e in range(1, ny):
         greet(on_y(e))
 
-    @pl.when(c > 0)
+    to_left = (c > 0) & (y == 0)
+    to_right = (c < cols - 1) & (y == ny - 1)
+
+    @pl.when(to_left)
     def _():
         greet((r, c - 1))
 
-    @pl.when(c < cols - 1)
+    @pl.when(to_right)
     def _():
         greet((r, c + 1))
 
@@ -139,7 +142,7 @@
         def _():
             greet((r + dr, c + dc))
 
-    beside_cols = (c > 0).astype(jnp.int32) + (c < cols - 1).astype(jnp.int32)
+    beside_cols = to_left.astype(jnp.int32) + to_right.astype(jnp.int32)
     pl.semaphore_wait(barrier, nz - 1 + ny - 1 + ROWS - 1 + beside_cols + across)
 
     def lib_z(size, d):

time: 58.7 us -> 58.7 us (level)
  no operation moved by 1% of the time
where the time goes in v7:
time: 58.7 us; the launch traced here: 58.6 us
  Pallas kernels  57.9 us (99%)
  between operations  0.64 us (1%)
    pallas_call x1, Pallas kernels, local(): pl.pallas_call(functools.partial(kernel, cols), out_shape=shapes, in_spec...  55.4 us
    pallas_call x1, Pallas kernels, local(): pl.pallas_call(finish, out_shape=shapes, in_specs=[hbm, hbm], out_specs=(...  2.5 us

profile of v7, /device:TPU:1, one launch (start us, length us, event | category | flops | bytes accessed | tf_op | source)
XLA Modules:
  0.0 58.6 jit_solution(11129148902285286919)
XLA Ops:
  0.6 55.4 %shard_map.59 = (f32[4096,128]{1,0:T(8,128)}, f32[224,128]{1,0:T(8,128)}) custom-call(f32[3584,128]{1,0:T(8,128)} %bitcast.4, f32[224,128]{1,0:T(8,128)} %lib_hbm.1, s32[8,2,32]{2,1,0:T(2,128)} %bitcast.5, s32[8,32]{1,0:T(8,128)} %counts_hbm.1), custom_call_target="tpu_custom_call" | custom-call | tf_op jit(solution)/shard_map/pallas_call | solution.py:595
  56.1 2.5 %shard_map.60 = (f32[4096,128]{1,0:T(8,128)}, f32[224,128]{1,0:T(8,128)}) custom-call(f32[4096,128]{1,0:T(8,128)} %get-tuple-element.6.abund_in, f32[224,128]{1,0:T(8,128)} %get-tuple-element.7.lgrad_in), custom_call_target="tpu_custom_call" | custom-call | tf_op jit(solution)/shard_map/pallas_call | solution.py:647
